TPU v7x, 32 devices: a whole 2x2x4 slice. The times are simulated.
32 devices in a mesh: rollout: 4 (over z), ctx: 8 (over y, x, core).
Axes of the slice: x: 2, y: 2, z: 4, core: 2. Of those that a mesh axis runs over, the one named last changes fastest.
Arguments:
- queries: bfloat16 [4, 1024, 4096], P('rollout', 'ctx'), may hold values from -6 to 6
- keys_values: bfloat16 [4, 2, 1024, 1024], P('rollout', None, 'ctx'), may hold values from -6 to 6
- image_rows: bfloat16 [4, 256, 6144], P('rollout', 'ctx'), may hold values from -6 to 6
- cotangent: bfloat16 [4, 1024, 4096], P('rollout', 'ctx'), may hold values from -96 to 96
- seq_image: int32 [4], replicated, may hold values from 0 to 3, as said below
- vis_start: int32 [4], P('rollout'), may hold values from 1 to 63
- comp_lengths: int32 [4, 16], P('rollout'), may hold values from 1 to 58, 704 in all within a row
Outputs:
- grad_queries: bfloat16 [4, 1024, 4096], P('rollout', 'ctx')
- grad_keys_values: bfloat16 [4, 2, 1024, 1024], P('rollout', None, 'ctx')
- grad_image: bfloat16 [4, 256, 6144], P('rollout', 'ctx')
Inputs may be any that keep to these rules, and one draw needn't show every extreme that they name: `seq_image`: each image belongs to exactly one group. The image's rows take positions vis_start to vis_start + 255 of the group's sequence. `comp_lengths`: each group's lengths sum to 704.
All inputs are finite; a program needn't handle non-finite values.
Results may differ from a plain program's by a relative error of at most 0.0068.
Values may be sent and summed in bfloat16 or wider, within the bound.
No kernel may reach another device: no remote copies, remote signals or barrier semaphores. Data moves between devices by JAX's collectives and lax.ppermute only.
A program may use at most 128 MiB of HBM per device.

v0:
```python
import functools
import itertools
import math

import jax
import jax.numpy as jnp
from jax import lax
from jax.experimental import pallas as pl
from jax.experimental.pallas import tpu as pltpu
from jax.sharding import PartitionSpec as P

HEADS = 32
KV_HEADS = 8
HEAD_DIM = 128
VIS = 256
PROMPT = 64
NCOMP = 16

RATIO = HEADS // KV_HEADS
PREFIX = VIS + PROMPT
Q_WIDTH = HEADS * HEAD_DIM
KV_WIDTH = KV_HEADS * HEAD_DIM
GROUP_WIDTH = RATIO * HEAD_DIM
IMAGE_BLOCK = 32
IMAGE_HALF = IMAGE_BLOCK // 2
KEY_CHUNK = 64
HIDDEN = -1e30
SCORE_SCALE = 1.0 / math.sqrt(HEAD_DIM)


def dot_nt(left, right):
    return lax.dot_general(
        left, right, (((1,), (1,)), ((), ())), preferred_element_type=jnp.float32
    )


def dot_nn(left, right):
    return lax.dot_general(
        left, right, (((1,), (0,)), ((), ())), preferred_element_type=jnp.float32
    )


def dot_tn(left, right):
    return lax.dot_general(
        left, right, (((0,), (0,)), ((), ())), preferred_element_type=jnp.float32
    )


def first_kernel(halo, seq_ref, vis_ref, image_ref, kv_ref, number_ref, *out_refs):
    ikv_ref, iq_ref, text_ref, tail_ref = out_refs
    groups = seq_ref.shape[0]
    group = lax.axis_index("rollout")
    here = lax.axis_index("ctx")
    images = [seq_ref[at] for at in range(groups)]
    number = jnp.int32(0)
    if groups == 4:
        for at, weight in enumerate((6, 2, 1)):
            for later in range(at + 1, groups):
                number = number + jnp.where(images[later] < images[at], weight, 0)
    place = jnp.int32(0)
    user = jnp.int32(0)
    for at in range(groups):
        place = place + jnp.where(group == at, images[at], 0)
        user = user + jnp.where(images[at] == group, at, 0)
    number_ref[0] = number
    number_ref[1] = place
    number_ref[2] = user
    iq_ref[...] = image_ref[0, :, :Q_WIDTH]
    ikv_ref[0] = image_ref[0, :, Q_WIDTH : Q_WIDTH + KV_WIDTH]
    ikv_ref[1] = image_ref[0, :, Q_WIDTH + KV_WIDTH :]
    tok_rows = kv_ref.shape[2]
    late_shard = VIS // tok_rows
    at = lax.broadcasted_iota(jnp.int32, (PROMPT, KV_WIDTH), 0)
    ahead = jnp.where(here == 0, 1, 0)
    behind = jnp.where(here == late_shard, 1, 0)
    kept = jnp.where(at < vis_ref[0], ahead, behind) == 1
    for part in range(2):
        rows = kv_ref[0, part, :PROMPT].astype(jnp.float32)
        text_ref[part] = jnp.where(kept, rows, 0.0).astype(jnp.bfloat16)
        tail_ref[part] = kv_ref[0, part, tok_rows - halo :]


def first_arrays(seq_image, vis_start, image_rows, keys_values, halo):
    rows = image_rows.shape[1]
    smem = pl.BlockSpec(memory_space=pltpu.SMEM)
    vmem = pl.BlockSpec(memory_space=pltpu.VMEM)
    tail = min(halo, keys_values.shape[2])
    return pl.pallas_call(
        functools.partial(first_kernel, tail),
        in_specs=[smem, smem, vmem, vmem],
        out_specs=[smem, vmem, vmem, vmem, vmem],
        out_shape=[
            jax.ShapeDtypeStruct((3,), jnp.int32),
            jax.ShapeDtypeStruct((2, rows, KV_WIDTH), jnp.bfloat16),
            jax.ShapeDtypeStruct((rows, Q_WIDTH), jnp.bfloat16),
            jax.ShapeDtypeStruct((2, PROMPT, KV_WIDTH), jnp.bfloat16),
            jax.ShapeDtypeStruct((2, tail, KV_WIDTH), jnp.bfloat16),
        ],
    )(seq_image, vis_start, image_rows, keys_values)


def segments(positions, length_ref):
    end = jnp.int32(PREFIX)
    segment = jnp.where(positions < PREFIX, 0, 1)
    for at in range(NCOMP):
        end = end + length_ref[0, at]
        segment = segment + jnp.where(positions >= end, 1, 0)
    return segment


def hide(visible):
    return jnp.where(visible, 0.0, HIDDEN)


def second_kernel(
    targets, tok_rows, image_rows, halo, vis_ref, length_ref, d_ref, kv_ref, t_ref, r_ref, *out_refs
):
    *window_refs, near_ref, whole_ref, image_ref, text_ref = out_refs
    here = lax.axis_index("ctx")
    ctx_size = lax.axis_size("ctx")
    row = lax.broadcasted_iota(jnp.int32, (IMAGE_BLOCK, tok_rows), 0)
    column = lax.broadcasted_iota(jnp.int32, (IMAGE_BLOCK, tok_rows), 1)
    place = jnp.where(row < image_rows, row, 1 << 20)
    picks = []
    for blocks in targets:
        for default, special in blocks:
            target = here if default is None else default
            for source, other in special:
                target = jnp.where(here == source, other, target)
            begin = vis_ref[0] + image_rows * target - tok_rows * here
            picks.append(jnp.where(column == place + begin, 1.0, 0.0).astype(jnp.bfloat16))
    picked = dot_nn(jnp.concatenate(picks, axis=0), d_ref[...]).astype(jnp.bfloat16)
    at = 0
    for window_ref in window_refs:
        window_ref[...] = picked[at : at + window_ref.shape[0]]
        at += window_ref.shape[0]

    @pl.when(pl.program_id(0) == 0)
    def _():
        vis = vis_ref[0]
        text = t_ref[...].astype(jnp.float32) + r_ref[...].astype(jnp.float32)
        if kv_ref.shape[1] == IMAGE_BLOCK:
            text_ref[:, :IMAGE_BLOCK] = kv_ref[...]
        text_ref[:, text_ref.shape[1] - PROMPT :] = text.astype(jnp.bfloat16)
        own_at = lax.broadcasted_iota(jnp.int32, (8, tok_rows), 1) + here * tok_rows
        own_segment = segments(own_at, length_ref)[:1]
        placeholder = (own_at >= vis) & (own_at < vis + VIS)
        own_row = jnp.where(placeholder, -1, own_at)
        whole_ref[...] = hide(own_row >= vis + VIS).astype(jnp.float32)
        own_row = own_row[:1]
        image_at = lax.broadcasted_iota(jnp.int32, (1, RATIO * IMAGE_BLOCK), 1) % IMAGE_BLOCK
        image_row = jnp.where(image_at < image_rows, vis + here * image_rows + image_at, -1)
        text_at = lax.broadcasted_iota(jnp.int32, (PROMPT, tok_rows), 0)
        text_at = text_at + jnp.where(text_at < vis, 0, VIS)
        near_ref[:PROMPT] = hide(text_at <= own_row)
        near_at = lax.broadcasted_iota(jnp.int32, (halo + tok_rows, tok_rows), 0)
        near_at = near_at + (here * tok_rows - halo)
        sees = (near_at <= own_row) & (near_at >= PREFIX)
        sees = sees & (segments(near_at, length_ref) == own_segment)
        near_ref[PROMPT:] = hide(sees)
        at = 0
        for core in range(2):
            for step in range(0, ctx_size, 2):
                begin = (here ^ (step + core)) * image_rows + vis
                shape = (image_rows, RATIO * IMAGE_BLOCK)
                block_at = lax.broadcasted_iota(jnp.int32, shape, 0) + begin
                image_ref[at : at + image_rows] = hide(block_at <= image_row)
                at += image_rows
        image_ref[VIS:] = hide(text_at <= image_row)


def second_arrays(vis_start, lengths, cotangent, image_kv, text, received, halo):
    tok_rows, width = cotangent.shape
    image_rows = image_kv.shape[1]
    text_rows = PROMPT + (image_rows if image_rows == IMAGE_BLOCK else 0)
    targets, rounds = window_targets(lax.axis_size("ctx"), tok_rows, image_rows)
    counts = [len(blocks) * IMAGE_BLOCK for blocks in targets]
    block = 2048
    spec = pl.BlockSpec
    smem = spec(memory_space=pltpu.SMEM)
    lanes = RATIO * IMAGE_BLOCK
    near = PROMPT + halo + tok_rows
    whole = lambda *shape: spec(shape, lambda at: (0,) * len(shape))
    out = pl.pallas_call(
        functools.partial(second_kernel, targets, tok_rows, image_rows, halo),
        grid=(width // block,),
        in_specs=[
            smem,
            smem,
            spec((tok_rows, block), lambda at: (0, at)),
            whole(2, image_rows, KV_WIDTH),
            whole(2, PROMPT, KV_WIDTH),
            whole(2, PROMPT, KV_WIDTH),
        ],
        out_specs=[spec((count, block), lambda at: (0, at)) for count in counts]
        + [
            whole(near, tok_rows),
            whole(8, tok_rows),
            whole(PREFIX, lanes),
            whole(2, text_rows, KV_WIDTH),
        ],
        out_shape=[jax.ShapeDtypeStruct((count, width), jnp.bfloat16) for count in counts]
        + [
            jax.ShapeDtypeStruct((near, tok_rows), jnp.float32),
            jax.ShapeDtypeStruct((8, tok_rows), jnp.float32),
            jax.ShapeDtypeStruct((PREFIX, lanes), jnp.float32),
            jax.ShapeDtypeStruct((2, text_rows, KV_WIDTH), jnp.bfloat16),
        ],
    )(vis_start, lengths, cotangent, image_kv, text, received)
    return out[: len(counts)], rounds, out[len(counts) :]


def first_products(parts, q_rows, d_rows):
    return [(dot_nt(keys, q_rows), dot_nt(values, d_rows)) for keys, values, _ in parts]


def chunks_of(rows):
    return [rows[at : at + KEY_CHUNK] for at in range(0, rows.shape[0], KEY_CHUNK)]


def fold_rows(rows, combine):
    folded = rows[:8]
    for at in range(8, rows.shape[0], 8):
        folded = combine(folded, rows[at : at + 8])
    return folded


def rows_backward(parts, products):
    scale = SCORE_SCALE * math.log2(math.e)
    scores, tops = [], []
    for (keys, values, bias), (raw, _) in zip(parts, products):
        one_row = bias.shape[0] == 1
        top = None
        for at, chunk in enumerate(chunks_of(raw)):
            chunk = chunk * scale
            if not one_row:
                chunk = chunk + bias[at * KEY_CHUNK : (at + 1) * KEY_CHUNK]
            scores.append((chunk, bias if one_row else None))
            folded = fold_rows(chunk, jnp.maximum)
            top = folded if top is None else jnp.maximum(top, folded)
        top = jnp.max(top, axis=0, keepdims=True)
        tops.append(top + bias if one_row else top)
    top = functools.reduce(jnp.maximum, tops)
    d_weights = [chunk for _, product in products for chunk in chunks_of(product)]
    total = mix = None
    kept = []
    for (chunk, bias), d_chunk in zip(scores, d_weights):
        terms = jnp.exp2(chunk + ((bias if bias is not None else 0.0) - top))
        folded = fold_rows(terms, jnp.add)
        total = folded if total is None else total + folded
        folded = fold_rows(terms * d_chunk, jnp.add)
        mix = folded if mix is None else mix + folded
        kept.append(terms)
    total = jnp.sum(total, axis=0, keepdims=True)
    mix = jnp.sum(mix, axis=0, keepdims=True)
    inverse = jnp.where(top > 0.5 * HIDDEN, 1.0 / total, 0.0)
    delta = mix * inverse
    weights, d_scores = [], []
    for terms, d_chunk in zip(kept, d_weights):
        chunk = terms * inverse
        weights.append(chunk.astype(jnp.bfloat16))
        d_scores.append((chunk * (d_chunk - delta)).astype(jnp.bfloat16))
    outcome = []
    for raw, _ in products:
        count = raw.shape[0] // KEY_CHUNK
        outcome.append(
            (jnp.concatenate(weights[:count], axis=0), jnp.concatenate(d_scores[:count], axis=0))
        )
        weights, d_scores = weights[count:], d_scores[count:]
    return outcome


def total_of(values):
    if len(values) == 1:
        return values[0]
    return sum(value.astype(jnp.float32) for value in values).astype(jnp.bfloat16)


def attend_kernel(
    block_rows,
    block_count,
    text_count,
    window_count,
    heads,
    halo,
    own,
    number_ref,
    near_ref,
    whole_ref,
    image_bias_ref,
    q_ref,
    d_ref,
    iq_ref,
    halo_ref,
    own_ref,
    *refs,
):
    block_refs, refs = refs[:block_count], refs[block_count:]
    text_refs, refs = refs[:text_count], refs[text_count:]
    window_refs, refs = refs[:window_count], refs[window_count:]
    dq_ref, *diq_refs, dmine_ref, dpair_ref, dhalo_ref, down_ref = refs
    text_refs = text_refs or [ref for ref in block_refs if ref.shape[1] > block_rows]
    near_bias = jnp.concatenate([near_ref[...]] * 2, axis=1)
    whole_bias = jnp.concatenate([whole_ref[:1]] * 2, axis=1)
    image_cotangent = total_of([ref[...] for ref in window_refs])
    image_queries = iq_ref[number_ref[1]]
    states = []
    units = []
    for head in range(heads):
        lanes = slice(head * HEAD_DIM, (head + 1) * HEAD_DIM)
        spans = [
            slice((head * RATIO + at) * HEAD_DIM, (head * RATIO + at + 1) * HEAD_DIM)
            for at in range(RATIO)
        ]
        visual, text, near = [], [], []
        for part in range(2):
            visual.append(
                jnp.concatenate([ref[part, :block_rows, lanes] for ref in block_refs], axis=0)
            )
            text.append(total_of([ref[part, -PROMPT:, lanes] for ref in text_refs]))
            near.append(
                jnp.concatenate(
                    [text[part], halo_ref[part, :, lanes], own_ref[0, part, :, lanes]], axis=0
                )
            )
        states.append((lanes, jnp.concatenate([visual[0], near[0]], axis=0).T, {}))
        own_parts = [(visual[0], visual[1], whole_bias), (near[0], near[1], near_bias)]
        for first in range(0, RATIO, 2):
            units.append((head, own_parts, q_ref, d_ref, spans[first : first + 2]))
        image_parts = [
            (visual[0], visual[1], image_bias_ref[:VIS]),
            (text[0], text[1], image_bias_ref[VIS:]),
        ]
        units.append((head, image_parts, image_queries, image_cotangent, spans))

    def begin(unit):
        _, parts, queries, cotangents, unit_spans = unit
        q_rows = jnp.concatenate([queries[:, span] for span in unit_spans], axis=0)
        d_rows = jnp.concatenate([cotangents[:, span] for span in unit_spans], axis=0)
        return q_rows, d_rows, first_products(parts, q_rows, d_rows)

    def finish(unit, begun):
        head, parts, _, _, unit_spans = unit
        lanes, keys_across, sums = states[head]
        q_rows, d_rows, products = begun
        outcome = rows_backward(parts, products)
        d_scores = jnp.concatenate([part[1] for part in outcome], axis=0)
        dq = dot_nn(keys_across[:, : d_scores.shape[0]], d_scores) * SCORE_SCALE
        dq = dq.astype(jnp.bfloat16).T
        rows = dq.shape[0] // len(unit_spans)
        for at, span in enumerate(unit_spans):
            if len(unit_spans) == 2:
                dq_ref[:, span] = dq[at * rows : (at + 1) * rows]
            else:
                for half, out_ref in enumerate(diq_refs):
                    place = at * rows + half * IMAGE_HALF
                    out_ref[:, span] = dq[place : place + IMAGE_HALF]
        for at, (weights, d_part) in enumerate(outcome):
            for kind, rows in ((0, dot_nn(d_part, q_rows)), (1, dot_nn(weights, d_rows))):
                count = rows.shape[0]
                earlier = sums.get((kind, at))
                if earlier is not None and count < earlier.shape[0]:
                    rows = jnp.concatenate([earlier[:count] + rows, earlier[count:]], axis=0)
                elif earlier is not None:
                    rows = earlier + rows
                sums[kind, at] = rows
        if len(unit_spans) == 2:
            return
        for part, scale in ((0, SCORE_SCALE), (1, 1.0)):
            of_visual = (sums[part, 0] * scale).astype(jnp.bfloat16)
            rest = sums[part, 1] * scale
            dmine_ref[part, :, lanes] = of_visual[: VIS // 2]
            dpair_ref[part, : VIS // 2, lanes] = of_visual[VIS // 2 :]
            dpair_ref[part, VIS // 2 :, lanes] = rest[:PROMPT].astype(jnp.bfloat16)
            dhalo_ref[part, :, lanes] = rest[PROMPT : PROMPT + halo].astype(jnp.bfloat16)
            down_ref[part, :, lanes] = rest[PROMPT + halo :]

    begun = begin(units[0])
    for at, unit in enumerate(units):
        later = begin(units[at + 1]) if at + 1 < len(units) else None
        finish(unit, begun)
        begun = later


def attend(
    number, masks, queries, cotangent, every_q, halo_kv, own_kv, blocks, texts, windows
):
    heads = 2
    near_bias, whole_bias, image_bias = masks
    own = queries.shape[0]
    halo = halo_kv.shape[1]
    groups = every_q.shape[0]
    columns = PREFIX + halo + own
    products = RATIO * (own * columns + IMAGE_BLOCK * PREFIX) * KV_HEADS
    spec = pl.BlockSpec
    kv_spec = lambda rows: spec((2, rows, heads * HEAD_DIM), lambda at: (0, 0, at))
    q_spec = lambda rows: spec((rows, heads * GROUP_WIDTH), lambda at: (0, at))
    whole = lambda rows: spec((rows, 128), lambda at: (0, 0))
    return pl.pallas_call(
        functools.partial(
            attend_kernel,
            VIS // len(blocks),
            len(blocks),
            len(texts),
            len(windows),
            heads,
            halo,
            own,
        ),
        grid=(KV_HEADS // heads,),
        in_specs=[
            spec(memory_space=pltpu.SMEM),
            whole(columns - VIS),
            whole(8),
            whole(PREFIX),
            q_spec(own),
            q_spec(own),
            spec((groups, IMAGE_BLOCK, heads * GROUP_WIDTH), lambda at: (0, 0, at)),
            kv_spec(halo),
            spec((1, 2, own, heads * HEAD_DIM), lambda at: (0, 0, 0, at)),
        ]
        + [kv_spec(block.shape[1]) for block in [*blocks, *texts]]
        + [q_spec(IMAGE_BLOCK) for _ in windows],
        out_specs=[
            q_spec(own),
            q_spec(IMAGE_HALF),
            q_spec(IMAGE_HALF),
            kv_spec(VIS // 2),
            kv_spec(VIS // 2 + PROMPT),
            kv_spec(halo),
            kv_spec(own),
        ],
        out_shape=[
            jax.ShapeDtypeStruct((own, Q_WIDTH), jnp.bfloat16),
            jax.ShapeDtypeStruct((IMAGE_HALF, Q_WIDTH), jnp.bfloat16),
            jax.ShapeDtypeStruct((IMAGE_HALF, Q_WIDTH), jnp.bfloat16),
            jax.ShapeDtypeStruct((2, VIS // 2, KV_WIDTH), jnp.bfloat16),
            jax.ShapeDtypeStruct((2, VIS // 2 + PROMPT, KV_WIDTH), jnp.bfloat16),
            jax.ShapeDtypeStruct((2, halo, KV_WIDTH), jnp.bfloat16),
            jax.ShapeDtypeStruct((2, own, KV_WIDTH), jnp.float32),
        ],
        cost_estimate=pl.CostEstimate(
            flops=10 * products * HEAD_DIM,
            bytes_accessed=12 * 1024 * 1024,
            transcendentals=products,
        ),
    )(
        number,
        near_bias,
        whole_bias,
        image_bias,
        queries,
        cotangent,
        every_q,
        halo_kv,
        own_kv,
        *blocks,
        *texts,
        *windows,
    )


def route(rows, number, back, beside=()):
    groups = lax.axis_size("rollout")
    arrays = [array for array, _ in beside]

    def move_beside(arrays):
        return [lax.ppermute(array, "ctx", pairs) for array, (_, pairs) in zip(arrays, beside)]

    if groups != 4:
        every = lax.all_gather(rows, "rollout", axis=0)
        picked = lax.dynamic_index_in_dim(every, number[2 if back else 1], 0, keepdims=False)
        return [picked] + move_beside(arrays)

    def branch(images):
        pairs = [(g, i) if back else (i, g) for g, i in enumerate(images)]
        return lambda rows, arrays: [lax.ppermute(rows, "rollout", pairs)] + move_beside(arrays)

    orders = itertools.permutations(range(groups))
    return lax.switch(number[0], [branch(images) for images in orders], rows, arrays)


def window_rounds(ctx_size, tok_rows, image_rows):
    rounds = []
    for target in range(ctx_size):
        lowest = (image_rows * target + 1) // tok_rows
        highest = (image_rows * target + image_rows - 1 + PROMPT - 1) // tok_rows
        for source in range(lowest, highest + 1):
            if source == target:
                continue
            for pairs in rounds:
                if all(s != source and t != target for s, t in pairs):
                    pairs.append((source, target))
                    break
            else:
                rounds.append([(source, target)])
    return rounds


def window_targets(ctx_size, tok_rows, image_rows):
    rounds = window_rounds(ctx_size, tok_rows, image_rows)
    if ctx_size != 8:
        return [[(None, [])]] + [[(None, pairs)] for pairs in rounds], rounds
    rounds = [[(0, 2), (1, 4), (2, 6)], [(0, 3), (1, 5), (2, 7)], [(1, 6)], [(1, 7)]]
    swapped = [(2, [(0, 1)]), (3, [])]
    return [[(None, [])]] + [[(None, pairs)] for pairs in rounds] + [swapped], rounds


def join_windows(own, one, two, swapped):
    here = lax.axis_index("ctx")
    wide = lambda rows: rows.astype(jnp.float32)
    near, far = swapped[:IMAGE_BLOCK], swapped[IMAGE_BLOCK:]
    sums = [
        jnp.where(here == 1, wide(own) + wide(near), wide(own)),
        jnp.where(here == 0, wide(one) + wide(near), wide(one)),
        jnp.where(here == 0, wide(two) + wide(far), wide(two)),
    ]
    return [part.astype(jnp.bfloat16) for part in sums]


def image_windows(windows, rounds):
    own, *sent = windows
    if lax.axis_size("ctx") == 8:
        one, two, three, four, swapped = sent
        late = [lax.ppermute(rows, "ctx", pairs) for rows, pairs in zip((three, four), rounds[2:])]
        own, one, two = on_device(join_windows, own, one, two, xor_permute(swapped, 1))
        return [own] + late + [
            lax.ppermute(rows, "ctx", pairs) for rows, pairs in zip((one, two), rounds)
        ]
    parts = [own] + [lax.ppermute(rows, "ctx", pairs) for rows, pairs in zip(sent, rounds)]
    return [sum(part.astype(jnp.float32) for part in parts).astype(jnp.bfloat16)]


def xor_pairs(step):
    return [(at, at ^ step) for at in range(lax.axis_size("ctx"))]


def xor_permute(rows, step):
    return lax.ppermute(rows, "ctx", xor_pairs(step))


def on_device(function, *arrays):
    if lax.axis_size("ctx") != 8:
        return function(*arrays)
    shapes = jax.eval_shape(function, *arrays)

    def kernel(*refs):
        for out_ref, value in zip(
            refs[len(arrays) :], function(*[ref[...] for ref in refs[: len(arrays)]])
        ):
            out_ref[...] = value

    def spec(array):
        *rows, width = array.shape
        return pl.BlockSpec((*rows, width // 2), lambda at: (0,) * len(rows) + (at,))

    return pl.pallas_call(
        kernel,
        grid=(2,),
        in_specs=[spec(array) for array in arrays],
        out_specs=[spec(shape) for shape in shapes],
        out_shape=[jax.ShapeDtypeStruct(shape.shape, shape.dtype) for shape in shapes],
        cost_estimate=pl.CostEstimate(flops=1, bytes_accessed=1, transcendentals=0),
    )(*arrays)


def text_strides(ctx_size, late_shard):
    strides = [1 << at for at in range(1, ctx_size.bit_length() - 1)]
    return [stride for stride in reversed(strides) if stride != late_shard]


def chip_steps(ctx_size):
    return list(range(2, ctx_size, 2))


def gather_prefix(image_kv, text, late_shard):
    ctx_size = lax.axis_size("ctx")
    steps = chip_steps(ctx_size)
    if ctx_size == 8:
        mine = [text, xor_permute(image_kv, 2), xor_permute(text, 4), xor_permute(image_kv, 6)]
        blocks = mine + [xor_permute(block, 1) for block in mine]
        return blocks, [blocks[at] for at in (0, 2, 4, 6)]
    mine = jnp.concatenate(
        [image_kv] + [xor_permute(image_kv, step) for step in steps], axis=1
    )
    return [mine, xor_permute(mine, 1)], list(spread_text(text, late_shard))


def split_sums(image_rows, steps, d_mine, d_pair, other):
    half = VIS // 2
    add = lambda one, two: one.astype(jnp.float32) + two.astype(jnp.float32)
    text = add(d_pair[:, half:], other[:, half:])
    out = []
    for at in range(len(steps) + 1):
        rows = slice(at * image_rows, (at + 1) * image_rows)
        sums = add(d_mine[:, rows], other[:, rows])
        if len(steps) == 3 and at in (1, 2):
            halves = text[2 - at]
            halves = jnp.stack([halves[: PROMPT // 2], halves[PROMPT // 2 :]])
            sums = jnp.concatenate([sums, halves], axis=1)
        out.append(sums.astype(jnp.bfloat16) if at else sums)
    return out + [text[0], text[1]]


def add_sums(image_rows, own, keys_text, values_text, *parts):
    texts = [values_text, keys_text]
    for at, part in enumerate(parts):
        own = own + part[:, :image_rows].astype(jnp.float32)
        if part.shape[1] > image_rows:
            rows = part[:, image_rows:].astype(jnp.float32)
            texts[at] = texts[at] + jnp.concatenate([rows[0], rows[1]], axis=0)
    return [part.astype(jnp.bfloat16) for part in (own, texts[1], texts[0])]


def spread_text(text, late_shard):
    for stride in text_strides(lax.axis_size("ctx"), late_shard):
        text = text + xor_permute(text, stride)
    return text, xor_permute(text, 1)


def collect_text(text, late_shard):
    for stride in reversed(text_strides(lax.axis_size("ctx"), late_shard)):
        moved = xor_permute(text.astype(jnp.bfloat16), stride)
        text = text.astype(jnp.float32) + moved.astype(jnp.float32)
    return text.astype(jnp.bfloat16)


def halo_cuts(tok_rows, halo):
    cuts = []
    left = halo
    while left > 0:
        cuts.append(min(left, tok_rows))
        left -= cuts[-1]
    return cuts


def halo_rows(tail, halo, tok_rows):
    ctx_size = lax.axis_size("ctx")
    parts = []
    for step, count in enumerate(halo_cuts(tok_rows, halo), 1):
        pairs = [(at, at + step) for at in range(ctx_size - step)]
        rows = tail if count == tail.shape[1] else tail[:, tail.shape[1] - count :]
        parts.insert(0, lax.ppermute(rows, "ctx", pairs))
    return jnp.concatenate(parts, axis=1) if len(parts) > 1 else parts[0]


def halo_parts(d_halo, tok_rows):
    ctx_size = lax.axis_size("ctx")
    cuts = halo_cuts(tok_rows, d_halo.shape[1])
    parts = []
    end = d_halo.shape[1]
    for step, count in enumerate(cuts, 1):
        rows = d_halo if len(cuts) == 1 else d_halo[:, end - count : end]
        parts.append((rows, [(at + step, at) for at in range(ctx_size - step)]))
        end -= count
    return parts


def last_kernel(part_count, vis_ref, dkv_ref, down_ref, *refs):
    text_refs, refs = refs[:4], refs[4:]
    part_refs = refs[:part_count]
    *dq_refs, image_ref, kv_ref = refs[part_count:]
    here = lax.axis_index("ctx")
    tok_rows = down_ref.shape[1]
    at = 0
    for dq_ref in dq_refs:
        image_ref[0, at : at + dq_ref.shape[0], :Q_WIDTH] = dq_ref[...]
        at += dq_ref.shape[0]
    image_ref[0, :, Q_WIDTH : Q_WIDTH + KV_WIDTH] = dkv_ref[0]
    image_ref[0, :, Q_WIDTH + KV_WIDTH :] = dkv_ref[1]
    at = lax.broadcasted_iota(jnp.int32, (PROMPT, KV_WIDTH), 0)
    ahead = jnp.where(here == 0, 1, 0)
    behind = jnp.where(here == VIS // tok_rows, 1, 0)
    kept = jnp.where(at < vis_ref[0], ahead, behind) == 1
    for part in range(2):
        text = text_refs[part][...].astype(jnp.float32)
        text = text + text_refs[2 + part][...].astype(jnp.float32)
        text = jnp.where(kept, text, 0.0)
        sums = down_ref[part] + jnp.concatenate(
            [text, jnp.zeros((tok_rows - PROMPT, KV_WIDTH), jnp.float32)], axis=0
        )
        for part_ref in part_refs:
            back = part_ref[part].astype(jnp.float32)
            if back.shape[0] < tok_rows:
                missing = jnp.zeros((tok_rows - back.shape[0], KV_WIDTH), jnp.float32)
                back = jnp.concatenate([missing, back], axis=0)
            sums = sums + back
        kv_ref[0, part] = sums.astype(jnp.bfloat16)


def last_arrays(vis_start, image_dq, image_dkv, d_own_kv, texts, parts):
    rows = image_dkv.shape[1]
    smem = pl.BlockSpec(memory_space=pltpu.SMEM)
    vmem = pl.BlockSpec(memory_space=pltpu.VMEM)
    return pl.pallas_call(
        functools.partial(last_kernel, len(parts)),
        in_specs=[smem] + [vmem] * (6 + len(parts) + len(image_dq)),
        out_specs=[vmem, vmem],
        out_shape=[
            jax.ShapeDtypeStruct((1, rows, Q_WIDTH + 2 * KV_WIDTH), jnp.bfloat16),
            jax.ShapeDtypeStruct((1,) + d_own_kv.shape, jnp.bfloat16),
        ],
    )(vis_start, image_dkv, d_own_kv, *texts, *parts, *image_dq)


def gather_queries(image_q):
    every = lax.all_gather(image_q, "rollout", axis=0)
    missing = IMAGE_BLOCK - every.shape[1]
    return jnp.pad(every, ((0, 0), (0, missing), (0, 0))) if missing else every


def per_device(queries, keys_values, image_rows, cotangent, seq_image, vis_start, comp_lengths):
    tok_rows = queries.shape[1]
    image_count = image_rows.shape[1]
    ctx_size = lax.axis_size("ctx")
    seq_len = tok_rows * ctx_size
    late_shard = VIS // tok_rows
    longest = 4 * (seq_len - PREFIX) // (3 * NCOMP)
    halo = -(-(longest - 1) // 64) * 64
    q_own, d_own = queries[0], cotangent[0]

    number, image_kv, image_q, text, tail = first_arrays(
        seq_image, vis_start, image_rows, keys_values, halo
    )
    every_q = gather_queries(image_q)
    image_kv, swapped = route(image_kv, number, False, [(text, xor_pairs(late_shard))])
    image_kv, d_later = lax.optimization_barrier((image_kv, d_own))
    windows, rounds, (*masks, text) = second_arrays(
        vis_start, comp_lengths, d_later, image_kv, text, swapped, halo
    )
    blocks, texts = gather_prefix(image_kv, text, late_shard)
    windows = image_windows(windows, rounds)
    halo_kv = halo_rows(tail, halo, tok_rows)

    grad_q, *d_image_q, d_mine, d_pair, d_halo, d_own_kv = attend(
        number,
        masks,
        q_own,
        d_own,
        every_q,
        halo_kv,
        keys_values,
        blocks,
        [] if ctx_size == 8 else texts,
        windows,
    )

    d_image_q = [
        half[: image_count - at * IMAGE_HALF]
        for at, half in enumerate(d_image_q)
        if at * IMAGE_HALF < image_count
    ]
    image_dq, other, *halo_back = route(
        d_image_q[0], number, True, [(d_pair, xor_pairs(1))] + halo_parts(d_halo, tok_rows)
    )
    image_dq = [image_dq]
    steps = chip_steps(ctx_size)
    own, *sent, keys_text, values_text = on_device(
        functools.partial(split_sums, image_count, steps), d_mine, d_pair, other
    )
    beside = [(rows, xor_pairs(step)) for rows, step in zip(sent, steps)]
    if len(d_image_q) > 1:
        second, *moved = route(d_image_q[1], number, True, beside)
        image_dq.append(second)
    else:
        moved = [lax.ppermute(rows, "ctx", pairs) for rows, pairs in beside]
    sums, keys_text, values_text = on_device(
        functools.partial(add_sums, image_count), own, keys_text, values_text, *moved
    )
    if ctx_size != 8:
        keys_text = collect_text(keys_text, late_shard)
        values_text = collect_text(values_text, late_shard)
    keys_step = late_shard
    values_step = 4 if ctx_size == 8 else late_shard
    image_dkv, *other_texts = route(
        sums,
        number,
        True,
        [(keys_text, xor_pairs(keys_step)), (values_text, xor_pairs(values_step))],
    )
    grad_image, grad_kv = last_arrays(
        vis_start,
        image_dq,
        image_dkv,
        d_own_kv,
        [keys_text, values_text, *other_texts],
        halo_back,
    )
    return (grad_q[None], grad_kv, grad_image)


def solution(mesh):
    placed = (
        P("rollout", "ctx", None),
        P("rollout", None, "ctx", None),
        P("rollout", "ctx", None),
        P("rollout", "ctx", None),
        P(),
        P("rollout"),
        P("rollout", None),
    )
    return jax.shard_map(
        per_device,
        mesh=mesh,
        in_specs=placed,
        out_specs=(
            P("rollout", "ctx", None),
            P("rollout", None, "ctx", None),
            P("rollout", "ctx", None),
        ),
        check_vma=False,
    )
```

profile of v0, /device:TPU:0, one launch (start us, length us, event | category | flops | bytes accessed | tf_op | source)
XLA Modules:
  0.0 112.2 jit_solution(3476042701974152506)
XLA Ops:
  7.9 2.0 %shard_map.94 = (s32[3]{0:T(128)}, bf16[2,32,1024]{2,1,0:T(8,128)(2,1)S(1)}, bf16[32,4096]{1,0:T(8,128)(2,1)}, bf16[2,64,1024]{2,1,0:T(8,128)(2,1)S(1)}, bf16[2,64,1024]{2,1,0:T(8,128)(2,1)}) custom-call(s32[4]{0:T(128)} %seq_ref.1, s32[1]{0:T(128)S(6)} %copy.298.vis_ref, bf16[1,32,6144]{2,1,0:T(8,128)(2,1)} %image_ref.1, bf16[1,2,128,1024]{3,2,1,0:T(8,128)(2,1)} %own_ref.1), custom_call_target="tpu_custom_call" | custom-call | tf_op jit(solution)/shard_map/pallas_call | solution.py:88
  9.9 0.6 copy-done.1
  10.6 9.4 %conditional.4 = (bf16[2,32,1024]{2,1,0:T(8,128)(2,1)}, bf16[2,64,1024]{2,1,0:T(8,128)(2,1)}) conditional(s32[]{:T(128)} %bitcast, (bf16[2,32,1024]{2,1,0:T(8,128)(2,1)S(1)}, bf16[2,64,1024]{2,1,0:T(8,128)(2,1)S(1)}) %tuple.369, (bf16[2,32,1024]{2,1,0:T(8,128)(2,1)S(1)}, ...), branch_computations={%region_0.0_spmd, %region_1.0_spmd, %region_2.0_spmd, %region_3.0_... | conditional | bytes 1572960 | solution.py:480
  10.6 3.0 %collective-permute-start.21 = (bf16[2,64,1024]{2,1,0:T(8,128)(2,1)S(1)}, bf16[2,64,1024]{2,1,0:T(8,128)(2,1)}, u32[]{:S(2)}, u32[]{:S(2)}) collective-permute-start(bf16[2,64,1024]{2,1,0:T(8,128)(2,1)S(1)} %get-tuple-element.597), channel_id=1, source_target_pairs={{0,2},{1,3},{2,0},{3,1},{4,6},{5,7},{6,4},{7,5},{8,10},{9,11},{10,... | collective-permute-start | bytes 786440 | tf_op jit(solution)/shard_map/cond/branch_10_fun/ppermute | solution.py:468
  13.6 2.6 %collective-permute-start.20 = (bf16[2,32,1024]{2,1,0:T(8,128)(2,1)S(1)}, bf16[2,32,1024]{2,1,0:T(8,128)(2,1)}, u32[]{:S(2)}, u32[]{:S(2)}) collective-permute-start(bf16[2,32,1024]{2,1,0:T(8,128)(2,1)S(1)} %get-tuple-element.596), channel_id=1, source_target_pairs={{8,0},{24,8},{0,16},{16,24},{9,1},{25,9},{1,17},{17,25},{10,2},{26... | collective-permute-start | bytes 393224 | tf_op jit(solution)/shard_map/cond/branch_10_fun/ppermute | solution.py:477
  16.2 2.5 %collective-permute-done.20 = bf16[2,32,1024]{2,1,0:T(8,128)(2,1)} collective-permute-done((bf16[2,32,1024]{2,1,0:T(8,128)(2,1)S(1)}, bf16[2,32,1024]{2,1,0:T(8,128)(2,1)}, u32[]{:S(2)}, u32[]{:S(2)}) %collective-permute-start.20) | collective-permute-done | bytes 131104 | tf_op jit(solution)/shard_map/cond/branch_10_fun/ppermute | solution.py:477
  18.7 1.3 %collective-permute-done.21 = bf16[2,64,1024]{2,1,0:T(8,128)(2,1)} collective-permute-done((bf16[2,64,1024]{2,1,0:T(8,128)(2,1)S(1)}, bf16[2,64,1024]{2,1,0:T(8,128)(2,1)}, u32[]{:S(2)}, u32[]{:S(2)}) %collective-permute-start.21) | collective-permute-done | bytes 262176 | tf_op jit(solution)/shard_map/cond/branch_10_fun/ppermute | solution.py:468
  20.0 3.5 %shard_map.95 = (bf16[32,4096]{1,0:T(8,128)(2,1)}, bf16[32,4096]{1,0:T(8,128)(2,1)}, bf16[32,4096]{1,0:T(8,128)(2,1)}, bf16[32,4096]{1,0:T(8,128)(2,1)}, bf16[32...) custom-call(s32[1]{0:T(128)S(6)} %copy.298.vis_ref, ...), custom_call_target="tpu_custom_call" | custom-call | tf_op jit(solution)/shard_map/pallas_call | solution.py:184
  23.6 1.8 %collective-permute-start.290 = (bf16[2,96,1024]{2,1,0:T(8,128)(2,1)}, bf16[2,96,1024]{2,1,0:T(8,128)(2,1)S(1)}, u32[]{:S(2)}, u32[]{:S(2)}) collective-permute-start(bf16[2,96,1024]{2,1,0:T(8,128)(2,1)} %get-tuple-element.928.refs_0_), channel_id=1, source_target_pairs={{0,4},{1,5},{2,6},{3,7},{4,0},{5,1},{6,2},{7,3},{8,12},{9,13},{10,... | collective-permute-start | bytes 1179656 | tf_op jit(solution)/shard_map/ppermute | solution.py:539
  25.4 1.5 %collective-permute-start.291 = (bf16[2,32,1024]{2,1,0:T(8,128)(2,1)}, bf16[2,32,1024]{2,1,0:T(8,128)(2,1)S(1)}, u32[]{:S(2)}, u32[]{:S(2)}) collective-permute-start(bf16[2,32,1024]{2,1,0:T(8,128)(2,1)} %get-tuple-element.921.kv_ref), channel_id=1, source_target_pairs={{0,6},{1,7},{2,4},{3,5},{4,2},{5,3},{6,0},{7,1},{8,14},{9,15},{10,... | collective-permute-start | bytes 393224 | tf_op jit(solution)/shard_map/ppermute | solution.py:539
  26.9 0.3 collective-permute-start.289
  27.1 5.8 %collective-permute-done.291.refs_3_ = bf16[2,32,1024]{2,1,0:T(8,128)(2,1)S(1)} collective-permute-done((bf16[2,32,1024]{2,1,0:T(8,128)(2,1)}, bf16[2,32,1024]{2,1,0:T(8,128)(2,1)S(1)}, u32[]{:S(2)}, u32[]{:S(2)}) %collective-permute-start.291) | collective-permute-done | bytes 131104 | tf_op jit(solution)/shard_map/ppermute | solution.py:539
  32.9 2.4 %collective-permute-start.288 = (bf16[2,64,1024]{2,1,0:T(8,128)(2,1)S(1)}, bf16[2,64,1024]{2,1,0:T(8,128)(2,1)S(1)}, u32[]{:S(2)}, u32[]{:S(2)}) collective-permute-start(bf16[2,64,1024]{2,1,0:T(8,128)(2,1)S(1)} %copy-done.5), channel_id=1, source_target_pairs={{0,1},{1,2},{2,3},{3,4},{4,5},{5,6},{6,7},{8,9},{9,10},{10,11},{11... | collective-permute-start | bytes 786440 | tf_op jit(solution)/shard_map/ppermute | solution.py:643
  35.4 0.7 collective-permute-start.297
  36.1 2.9 %collective-permute-start.293 = (bf16[2,32,1024]{2,1,0:T(8,128)(2,1)S(1)}, bf16[2,32,1024]{2,1,0:T(8,128)(2,1)S(1)}, u32[]{:S(2)}, u32[]{:S(2)}) collective-permute-start(bf16[2,32,1024]{2,1,0:T(8,128)(2,1)S(1)} %collective-permute-done.289.refs_1_), channel_id=1, source_target_pairs={{0,1},{1,0},{2,3},{3,2},{4,5},{5,4},{6,7},{7,6},{8,9},{9,8},{10,11... | collective-permute-start | bytes 393224 | tf_op jit(solution)/shard_map/ppermute | solution.py:539
  38.9 1.4 %collective-permute-done.290.refs_2_ = bf16[2,96,1024]{2,1,0:T(8,128)(2,1)S(1)} collective-permute-done((bf16[2,96,1024]{2,1,0:T(8,128)(2,1)}, bf16[2,96,1024]{2,1,0:T(8,128)(2,1)S(1)}, u32[]{:S(2)}, u32[]{:S(2)}) %collective-permute-start.290) | collective-permute-done | bytes 393248 | tf_op jit(solution)/shard_map/ppermute | solution.py:539
  40.3 0.5 collective-permute-start.294
  40.9 0.3 copy-done
  41.2 2.2 %shard_map.96 = (bf16[32,4096]{1,0:T(8,128)(2,1)}, bf16[32,4096]{1,0:T(8,128)(2,1)}, bf16[32,4096]{1,0:T(8,128)(2,1)}) custom-call(bf16[32,4096]{1,0:T(8,128)(2,1)} %get-tuple-element.929.refs_0_, bf16[32,4096]{1,0:T(8,128)(2,1)} %get-tuple-element.930.refs_1_, bf16[32,4096]{1,0:T(8,128)(2,1)} %get-tuple-element.931.refs_2_, bf16[64,4096]{1,0:T(8,128)(2,1)} %copy-done), custom_call_target="tpu_custom_call" | custom-call | flops 1 | bytes 1 | tf_op jit(solution)/shard_map/pallas_call | solution.py:557
  43.4 0.6 copy-done.16
  44.0 0.7 collective-permute-start.298
  44.7 1.5 %collective-permute-start.299 = (bf16[32,4096]{1,0:T(8,128)(2,1)}, bf16[32,4096]{1,0:T(8,128)(2,1)S(1)}, u32[]{:S(2)}, u32[]{:S(2)}) collective-permute-start(bf16[32,4096]{1,0:T(8,128)(2,1)} %get-tuple-element.936), channel_id=1, source_target_pairs={{0,2},{1,4},{2,6},{8,10},{9,12},{10,14},{16,18},{17,20},{18,22},{2... | collective-permute-start | bytes 786440 | tf_op jit(solution)/shard_map/ppermute | solution.py:528
  46.2 1.3 %collective-permute-start.300 = (bf16[32,4096]{1,0:T(8,128)(2,1)}, bf16[32,4096]{1,0:T(8,128)(2,1)S(1)}, u32[]{:S(2)}, u32[]{:S(2)}) collective-permute-start(bf16[32,4096]{1,0:T(8,128)(2,1)} %get-tuple-element.937), channel_id=1, source_target_pairs={{0,3},{1,5},{2,7},{8,11},{9,13},{10,15},{16,19},{17,21},{18,23},{2... | collective-permute-start | bytes 786440 | tf_op jit(solution)/shard_map/ppermute | solution.py:528
  47.6 5.1 %collective-permute-done.299.refs_11_ = bf16[32,4096]{1,0:T(8,128)(2,1)S(1)} collective-permute-done((bf16[32,4096]{1,0:T(8,128)(2,1)}, bf16[32,4096]{1,0:T(8,128)(2,1)S(1)}, u32[]{:S(2)}, u32[]{:S(2)}) %collective-permute-start.299) | collective-permute-done | bytes 262176 | tf_op jit(solution)/shard_map/ppermute | solution.py:528
  52.7 2.8 %collective-permute-done.300.refs_12_ = bf16[32,4096]{1,0:T(8,128)(2,1)S(1)} collective-permute-done((bf16[32,4096]{1,0:T(8,128)(2,1)}, bf16[32,4096]{1,0:T(8,128)(2,1)S(1)}, u32[]{:S(2)}, u32[]{:S(2)}) %collective-permute-start.300) | collective-permute-done | bytes 262176 | tf_op jit(solution)/shard_map/ppermute | solution.py:528
  55.6 0.6 copy-done.11
  56.2 0.2 copy-done.4
  56.4 12.7 %shard_map.97 = (bf16[128,4096]{1,0:T(8,128)(2,1)}, bf16[16,4096]{1,0:T(8,128)(2,1)}, bf16[16,4096]{1,0:T(8,128)(2,1)}, bf16[2,128,1024]{2,1,0:T(8,128)(2,1)}, b...) custom-call(s32[3]{0:T(128)} %get-tuple-element.916.number_ref, ...), custom_call_target="tpu_custom_call" | custom-call | flops 3103784960 | bytes 12582912 | tf_op jit(solution)/shard_map/pallas_call | solution.py:399
  69.1 8.9 %conditional.5 = (bf16[16,4096]{1,0:T(8,128)(2,1)}, bf16[2,192,1024]{2,1,0:T(8,128)(2,1)}, bf16[2,64,1024]{2,1,0:T(8,128)(2,1)}) conditional(s32[]{:T(128)} %bitcast, (bf16[16,4096]{1,0:T(8,128)(2,1)}, bf16[2,192,1024]{2,1,0:T(8,128)(2,1)S(1)}, bf16[2,64,1024]{2,1,0:T(8,128)(2,1)S(1)}) %tuple.371, ...), branch_computations={%region_24.0_spmd, %region_25.0_spmd, %region_26.0_spmd, %region_2... | conditional | bytes 4718736 | solution.py:480
  69.3 1.3 %collective-permute-start.80 = (bf16[2,64,1024]{2,1,0:T(8,128)(2,1)S(1)}, bf16[2,64,1024]{2,1,0:T(8,128)(2,1)}, u32[]{:S(2)}, u32[]{:S(2)}) collective-permute-start(bf16[2,64,1024]{2,1,0:T(8,128)(2,1)S(1)} %get-tuple-element.656), channel_id=1, source_target_pairs={{1,0},{2,1},{3,2},{4,3},{5,4},{6,5},{7,6},{9,8},{10,9},{11,10},{12... | collective-permute-start | bytes 786440 | tf_op jit(solution)/shard_map/cond/branch_10_fun/ppermute | solution.py:468
  70.6 1.6 %collective-permute-start.78 = (bf16[16,4096]{1,0:T(8,128)(2,1)}, bf16[16,4096]{1,0:T(8,128)(2,1)}, u32[]{:S(2)}, u32[]{:S(2)}) collective-permute-start(bf16[16,4096]{1,0:T(8,128)(2,1)} %get-tuple-element.654), channel_id=1, source_target_pairs={{0,8},{8,24},{16,0},{24,16},{1,9},{9,25},{17,1},{25,17},{2,10},{10... | collective-permute-start | bytes 393224 | tf_op jit(solution)/shard_map/cond/branch_10_fun/ppermute | solution.py:477
  72.2 5.8 %collective-permute-done.78 = bf16[16,4096]{1,0:T(8,128)(2,1)} collective-permute-done((bf16[16,4096]{1,0:T(8,128)(2,1)}, bf16[16,4096]{1,0:T(8,128)(2,1)}, u32[]{:S(2)}, u32[]{:S(2)}) %collective-permute-start.78) | collective-permute-done | bytes 131104 | tf_op jit(solution)/shard_map/cond/branch_10_fun/ppermute | solution.py:477
  78.1 2.2 %shard_map.98 = (f32[2,32,1024]{2,1,0:T(8,128)}, bf16[2,64,1024]{2,1,0:T(8,128)(2,1)S(1)}, bf16[2,64,1024]{2,1,0:T(8,128)(2,1)S(1)}, bf16[2,32,1024]{2,1,0:T(8,1...) custom-call(bf16[2,128,1024]{2,1,0:T(8,128)(2,1)} %get-tuple-element.939.refs_0_, ...), custom_call_target="tpu_custom_call" | custom-call | flops 1 | bytes 1 | tf_op jit(solution)/shard_map/pallas_call | solution.py:557
  80.2 13.6 %conditional.6 = (bf16[16,4096]{1,0:T(8,128)(2,1)}, bf16[2,64,1024]{2,1,0:T(8,128)(2,1)}, bf16[2,64,1024]{2,1,0:T(8,128)(2,1)}, bf16[2,32,1024]{2,1,0:T(8,128)(2,1)}) conditional(s32[]{:T(128)} %bitcast, (bf16[16,4096]{1,0:T(8,128)(2,1)S(1)}, bf16[2,64,1024]{2,1,0:T(8,128)(2,1)S(1)}, ...), branch_computations={%region_48.0_spmd, %region_49.0_spmd, %region_50.0_spmd, %region_5... | conditional | bytes 3145920 | solution.py:480
  80.2 2.5 %collective-permute-start.161 = (bf16[2,64,1024]{2,1,0:T(8,128)(2,1)S(1)}, bf16[2,64,1024]{2,1,0:T(8,128)(2,1)}, u32[]{:S(2)}, u32[]{:S(2)}) collective-permute-start(bf16[2,64,1024]{2,1,0:T(8,128)(2,1)S(1)} %get-tuple-element.737), channel_id=1, source_target_pairs={{0,2},{1,3},{2,0},{3,1},{4,6},{5,7},{6,4},{7,5},{8,10},{9,11},{10,... | collective-permute-start | bytes 786440 | tf_op jit(solution)/shard_map/cond/branch_10_fun/ppermute | solution.py:468
  82.8 1.8 %collective-permute-start.162 = (bf16[2,64,1024]{2,1,0:T(8,128)(2,1)S(1)}, bf16[2,64,1024]{2,1,0:T(8,128)(2,1)}, u32[]{:S(2)}, u32[]{:S(2)}) collective-permute-start(bf16[2,64,1024]{2,1,0:T(8,128)(2,1)S(1)} %get-tuple-element.738), channel_id=1, source_target_pairs={{0,4},{1,5},{2,6},{3,7},{4,0},{5,1},{6,2},{7,3},{8,12},{9,13},{10,... | collective-permute-start | bytes 786440 | tf_op jit(solution)/shard_map/cond/branch_10_fun/ppermute | solution.py:468
  84.6 0.8 collective-permute-start.160
  85.4 5.1 %collective-permute-done.160 = bf16[16,4096]{1,0:T(8,128)(2,1)} collective-permute-done((bf16[16,4096]{1,0:T(8,128)(2,1)S(1)}, bf16[16,4096]{1,0:T(8,128)(2,1)}, u32[]{:S(2)}, u32[]{:S(2)}) %collective-permute-start.160) | collective-permute-done | bytes 131104 | tf_op jit(solution)/shard_map/cond/branch_10_fun/ppermute | solution.py:477
  90.5 3.1 %collective-permute-done.163 = bf16[2,32,1024]{2,1,0:T(8,128)(2,1)} collective-permute-done((bf16[2,32,1024]{2,1,0:T(8,128)(2,1)S(1)}, bf16[2,32,1024]{2,1,0:T(8,128)(2,1)}, u32[]{:S(2)}, u32[]{:S(2)}) %collective-permute-start.163) | collective-permute-done | bytes 131104 | tf_op jit(solution)/shard_map/cond/branch_10_fun/ppermute | solution.py:468
  93.6 0.2 collective-permute-done.162
  93.8 1.5 %shard_map.99 = (bf16[2,32,1024]{2,1,0:T(8,128)(2,1)S(1)}, bf16[64,1024]{1,0:T(8,128)(2,1)S(1)}, bf16[64,1024]{1,0:T(8,128)(2,1)S(1)}) custom-call(f32[2,32,1024]{2,1,0:T(8,128)} %get-tuple-element.944.refs_0_, f32[64,1024]{1,0:T(8,128)} %get-tuple-element.945.refs_1_, f32[64,1024]{1,0:T(8,128)} %get-tuple-element.946.refs_2_, ...), custom_call_target="tpu_custom_call" | custom-call | flops 1 | bytes 1 | tf_op jit(solution)/shard_map/pallas_call | solution.py:557
  95.3 7.7 %conditional.7 = (bf16[2,32,1024]{2,1,0:T(8,128)(2,1)}, bf16[64,1024]{1,0:T(8,128)(2,1)}, bf16[64,1024]{1,0:T(8,128)(2,1)}) conditional(s32[]{:T(128)} %bitcast, (bf16[2,32,1024]{2,1,0:T(8,128)(2,1)S(1)}, bf16[64,1024]{1,0:T(8,128)(2,1)S(1)}, bf16[64,1024]{1,0:T(8,128)(2,1)S(1)}) %shard_map.99, ...), branch_computations={%region_72.0_spmd, %region_73.0_spmd, %region_74.0_spmd, %region_7... | conditional | bytes 1573008 | solution.py:480
  95.3 1.1 collective-permute-start.246
  96.4 1.5 %collective-permute-start.247 = (bf16[64,1024]{1,0:T(8,128)(2,1)S(1)}, bf16[64,1024]{1,0:T(8,128)(2,1)}, u32[]{:S(2)}, u32[]{:S(2)}) collective-permute-start(bf16[64,1024]{1,0:T(8,128)(2,1)S(1)} %get-tuple-element.823), channel_id=1, source_target_pairs={{0,2},{1,3},{2,0},{3,1},{4,6},{5,7},{6,4},{7,5},{8,10},{9,11},{10,... | collective-permute-start | bytes 393224 | tf_op jit(solution)/shard_map/cond/branch_10_fun/ppermute | solution.py:468
  97.9 0.6 collective-permute-start.248
  98.5 2.8 %collective-permute-done.246 = bf16[2,32,1024]{2,1,0:T(8,128)(2,1)} collective-permute-done((bf16[2,32,1024]{2,1,0:T(8,128)(2,1)S(1)}, bf16[2,32,1024]{2,1,0:T(8,128)(2,1)}, u32[]{:S(2)}, u32[]{:S(2)}) %collective-permute-start.246) | collective-permute-done | bytes 131104 | tf_op jit(solution)/shard_map/cond/branch_10_fun/ppermute | solution.py:477
  101.5 1.5 %collective-permute-done.248 = bf16[64,1024]{1,0:T(8,128)(2,1)} collective-permute-done((bf16[64,1024]{1,0:T(8,128)(2,1)S(1)}, bf16[64,1024]{1,0:T(8,128)(2,1)}, u32[]{:S(2)}, u32[]{:S(2)}) %collective-permute-start.248) | collective-permute-done | bytes 131104 | tf_op jit(solution)/shard_map/cond/branch_10_fun/ppermute | solution.py:468
  103.0 2.4 %shard_map.100 = (bf16[1,32,6144]{2,1,0:T(8,128)(2,1)}, bf16[1,2,128,1024]{3,2,1,0:T(8,128)(2,1)}) custom-call(s32[1]{0:T(128)S(6)} %copy.298.vis_ref, bf16[2,32,1024]{2,1,0:T(8,128)(2,1)} %get-tuple-element.954.dkv_ref, f32[2,128,1024]{2,1,0:T(8,128)} %get-tuple-element.955.down_ref, bf16[64,1024]{1,0:T(8,128)(2,1)S(1)} %get-tuple-element.956.refs_0_, ...), custom_call_target="tpu_custom_call" | custom-call | tf_op jit(solution)/shard_map/pallas_call | solution.py:695
  (50 shorter events, 0.5 us)
Async XLA Ops:
  7.2 48.4 %all-gather.3.cloned.1.call-start = ((), (), s32[]{:S(2)}) async-start(), calls=%async_computation | async-start | bytes 1310720 | tf_op jit(solution)/shard_map/all_gather | solution.py:707
  9.9 0.6 copy-start.1
  10.6 9.4 %collective-permute-start.21 = (bf16[2,64,1024]{2,1,0:T(8,128)(2,1)S(1)}, bf16[2,64,1024]{2,1,0:T(8,128)(2,1)}, u32[]{:S(2)}, u32[]{:S(2)}) collective-permute-start(bf16[2,64,1024]{2,1,0:T(8,128)(2,1)S(1)} %get-tuple-element.597), channel_id=1, source_target_pairs={{0,2},{1,3},{2,0},{3,1},{4,6},{5,7},{6,4},{7,5},{8,10},{9,11},{10,... | collective-permute-start | bytes 786440 | tf_op jit(solution)/shard_map/cond/branch_10_fun/ppermute | solution.py:468
  13.6 5.1 %collective-permute-start.20 = (bf16[2,32,1024]{2,1,0:T(8,128)(2,1)S(1)}, bf16[2,32,1024]{2,1,0:T(8,128)(2,1)}, u32[]{:S(2)}, u32[]{:S(2)}) collective-permute-start(bf16[2,32,1024]{2,1,0:T(8,128)(2,1)S(1)} %get-tuple-element.596), channel_id=1, source_target_pairs={{8,0},{24,8},{0,16},{16,24},{9,1},{25,9},{1,17},{17,25},{10,2},{26... | collective-permute-start | bytes 393224 | tf_op jit(solution)/shard_map/cond/branch_10_fun/ppermute | solution.py:477
  20.0 12.9 %copy-start.5 = (bf16[2,64,1024]{2,1,0:T(8,128)(2,1)S(1)}, bf16[2,64,1024]{2,1,0:T(8,128)(2,1)}, u32[]{:S(2)}) copy-start(bf16[2,64,1024]{2,1,0:T(8,128)(2,1)} %get-tuple-element.927) | copy-start | bytes 786436
  23.5 16.8 %collective-permute-start.296 = (bf16[64,4096]{1,0:T(8,128)(2,1)}, bf16[64,4096]{1,0:T(8,128)(2,1)S(1)}, u32[]{:S(2)}, u32[]{:S(2)}) collective-permute-start(bf16[64,4096]{1,0:T(8,128)(2,1)} %get-tuple-element.932), channel_id=1, source_target_pairs={{0,1},{1,0},{2,3},{3,2},{4,5},{5,4},{6,7},{7,6},{8,9},{9,8},{10,11... | collective-permute-start | bytes 1572872 | tf_op jit(solution)/shard_map/ppermute | solution.py:539
  23.6 16.7 %collective-permute-start.290 = (bf16[2,96,1024]{2,1,0:T(8,128)(2,1)}, bf16[2,96,1024]{2,1,0:T(8,128)(2,1)S(1)}, u32[]{:S(2)}, u32[]{:S(2)}) collective-permute-start(bf16[2,96,1024]{2,1,0:T(8,128)(2,1)} %get-tuple-element.928.refs_0_), channel_id=1, source_target_pairs={{0,4},{1,5},{2,6},{3,7},{4,0},{5,1},{6,2},{7,3},{8,12},{9,13},{10,... | collective-permute-start | bytes 1179656 | tf_op jit(solution)/shard_map/ppermute | solution.py:539
  25.4 7.5 %collective-permute-start.291 = (bf16[2,32,1024]{2,1,0:T(8,128)(2,1)}, bf16[2,32,1024]{2,1,0:T(8,128)(2,1)S(1)}, u32[]{:S(2)}, u32[]{:S(2)}) collective-permute-start(bf16[2,32,1024]{2,1,0:T(8,128)(2,1)} %get-tuple-element.921.kv_ref), channel_id=1, source_target_pairs={{0,6},{1,7},{2,4},{3,5},{4,2},{5,3},{6,0},{7,1},{8,14},{9,15},{10,... | collective-permute-start | bytes 393224 | tf_op jit(solution)/shard_map/ppermute | solution.py:539
  26.9 8.5 %collective-permute-start.289 = (bf16[2,32,1024]{2,1,0:T(8,128)(2,1)}, bf16[2,32,1024]{2,1,0:T(8,128)(2,1)S(1)}, u32[]{:S(2)}, u32[]{:S(2)}) collective-permute-start(bf16[2,32,1024]{2,1,0:T(8,128)(2,1)} %get-tuple-element.921.kv_ref), channel_id=1, source_target_pairs={{0,2},{1,3},{2,0},{3,1},{4,6},{5,7},{6,4},{7,5},{8,10},{9,11},{10,... | collective-permute-start | bytes 393224 | tf_op jit(solution)/shard_map/ppermute | solution.py:539
  32.9 7.9 %copy-start.13 = (bf16[2,32,1024]{2,1,0:T(8,128)(2,1)}, bf16[2,32,1024]{2,1,0:T(8,128)(2,1)S(1)}, u32[]{:S(2)}) copy-start(bf16[2,32,1024]{2,1,0:T(8,128)(2,1)S(1)} %collective-permute-done.291.refs_3_) | copy-start | bytes 393220
  32.9 3.1 %collective-permute-start.295 = (bf16[2,32,1024]{2,1,0:T(8,128)(2,1)S(1)}, bf16[2,32,1024]{2,1,0:T(8,128)(2,1)S(1)}, u32[]{:S(2)}, u32[]{:S(2)}) collective-permute-start(bf16[2,32,1024]{2,1,0:T(8,128)(2,1)S(1)} %collective-permute-done.291.refs_3_), channel_id=1, source_target_pairs={{0,1},{1,0},{2,3},{3,2},{4,5},{5,4},{6,7},{7,6},{8,9},{9,8},{10,11... | collective-permute-start | bytes 393224 | tf_op jit(solution)/shard_map/ppermute | solution.py:539
  32.9 11.8 %collective-permute-start.288 = (bf16[2,64,1024]{2,1,0:T(8,128)(2,1)S(1)}, bf16[2,64,1024]{2,1,0:T(8,128)(2,1)S(1)}, u32[]{:S(2)}, u32[]{:S(2)}) collective-permute-start(bf16[2,64,1024]{2,1,0:T(8,128)(2,1)S(1)} %copy-done.5), channel_id=1, source_target_pairs={{0,1},{1,2},{2,3},{3,4},{4,5},{5,6},{6,7},{8,9},{9,10},{10,11},{11... | collective-permute-start | bytes 786440 | tf_op jit(solution)/shard_map/ppermute | solution.py:643
  35.4 8.0 %copy-start.14 = (bf16[2,32,1024]{2,1,0:T(8,128)(2,1)}, bf16[2,32,1024]{2,1,0:T(8,128)(2,1)S(1)}, u32[]{:S(2)}) copy-start(bf16[2,32,1024]{2,1,0:T(8,128)(2,1)S(1)} %collective-permute-done.289.refs_1_) | copy-start | bytes 393220
  35.4 10.8 %collective-permute-start.297 = (bf16[32,4096]{1,0:T(8,128)(2,1)}, bf16[32,4096]{1,0:T(8,128)(2,1)S(1)}, u32[]{:S(2)}, u32[]{:S(2)}) collective-permute-start(bf16[32,4096]{1,0:T(8,128)(2,1)} %get-tuple-element.934), channel_id=1, source_target_pairs={{1,6},{9,14},{17,22},{25,30}} | collective-permute-start | bytes 786440 | tf_op jit(solution)/shard_map/ppermute | solution.py:525
  36.1 2.9 %copy-start.15 = (bf16[2,32,1024]{2,1,0:T(8,128)(2,1)}, bf16[2,32,1024]{2,1,0:T(8,128)(2,1)S(1)}, u32[]{:S(2)}) copy-start(bf16[2,32,1024]{2,1,0:T(8,128)(2,1)S(1)} %collective-permute-done.295.refs_7_) | copy-start | bytes 393220
  36.1 7.3 %collective-permute-start.293 = (bf16[2,32,1024]{2,1,0:T(8,128)(2,1)S(1)}, bf16[2,32,1024]{2,1,0:T(8,128)(2,1)S(1)}, u32[]{:S(2)}, u32[]{:S(2)}) collective-permute-start(bf16[2,32,1024]{2,1,0:T(8,128)(2,1)S(1)} %collective-permute-done.289.refs_1_), channel_id=1, source_target_pairs={{0,1},{1,0},{2,3},{3,2},{4,5},{5,4},{6,7},{7,6},{8,9},{9,8},{10,11... | collective-permute-start | bytes 393224 | tf_op jit(solution)/shard_map/ppermute | solution.py:539
  40.3 15.2 %copy-start.2 = (bf16[2,96,1024]{2,1,0:T(8,128)(2,1)}, bf16[2,96,1024]{2,1,0:T(8,128)(2,1)S(1)}, u32[]{:S(2)}) copy-start(bf16[2,96,1024]{2,1,0:T(8,128)(2,1)S(1)} %collective-permute-done.290.refs_2_) | copy-start | bytes 1179652
  40.3 7.2 %collective-permute-start.292 = (bf16[2,96,1024]{2,1,0:T(8,128)(2,1)}, bf16[2,96,1024]{2,1,0:T(8,128)(2,1)S(1)}, u32[]{:S(2)}, u32[]{:S(2)}) collective-permute-start(bf16[2,96,1024]{2,1,0:T(8,128)(2,1)} %get-tuple-element.928.refs_0_), channel_id=1, source_target_pairs={{0,1},{1,0},{2,3},{3,2},{4,5},{5,4},{6,7},{7,6},{8,9},{9,8},{10,11... | collective-permute-start | bytes 1179656 | tf_op jit(solution)/shard_map/ppermute | solution.py:539
  40.3 0.8 copy-start
  40.3 15.2 %collective-permute-start.294 = (bf16[2,96,1024]{2,1,0:T(8,128)(2,1)S(1)}, bf16[2,96,1024]{2,1,0:T(8,128)(2,1)S(1)}, u32[]{:S(2)}, u32[]{:S(2)}) collective-permute-start(bf16[2,96,1024]{2,1,0:T(8,128)(2,1)S(1)} %collective-permute-done.290.refs_2_), channel_id=1, source_target_pairs={{0,1},{1,0},{2,3},{3,2},{4,5},{5,4},{6,7},{7,6},{8,9},{9,8},{10,11... | collective-permute-start | bytes 1179656 | tf_op jit(solution)/shard_map/ppermute | solution.py:539
  41.2 2.8 %copy-start.7 = (bf16[32,4096]{1,0:T(8,128)(2,1)S(1)}, bf16[32,4096]{1,0:T(8,128)(2,1)}, u32[]{:S(2)}) copy-start(bf16[32,4096]{1,0:T(8,128)(2,1)} %get-tuple-element.935) | copy-start | bytes 786436
  43.3 0.7 copy-start.16
  44.0 3.5 %collective-permute-start.298 = (bf16[32,4096]{1,0:T(8,128)(2,1)S(1)}, bf16[32,4096]{1,0:T(8,128)(2,1)S(1)}, u32[]{:S(2)}, u32[]{:S(2)}) collective-permute-start(bf16[32,4096]{1,0:T(8,128)(2,1)S(1)} %copy-done.7), channel_id=1, source_target_pairs={{1,7},{9,15},{17,23},{25,31}} | collective-permute-start | bytes 786440 | tf_op jit(solution)/shard_map/ppermute | solution.py:525
  44.7 10.9 %copy-start.6 = (bf16[2,64,1024]{2,1,0:T(8,128)(2,1)}, bf16[2,64,1024]{2,1,0:T(8,128)(2,1)S(1)}, u32[]{:S(2)}) copy-start(bf16[2,64,1024]{2,1,0:T(8,128)(2,1)S(1)} %collective-permute-done.288.halo_ref) | copy-start | bytes 786436
  44.7 8.0 %collective-permute-start.299 = (bf16[32,4096]{1,0:T(8,128)(2,1)}, bf16[32,4096]{1,0:T(8,128)(2,1)S(1)}, u32[]{:S(2)}, u32[]{:S(2)}) collective-permute-start(bf16[32,4096]{1,0:T(8,128)(2,1)} %get-tuple-element.936), channel_id=1, source_target_pairs={{0,2},{1,4},{2,6},{8,10},{9,12},{10,14},{16,18},{17,20},{18,22},{2... | collective-permute-start | bytes 786440 | tf_op jit(solution)/shard_map/ppermute | solution.py:528
  46.2 9.4 %copy-start.8 = (bf16[32,4096]{1,0:T(8,128)(2,1)}, bf16[32,4096]{1,0:T(8,128)(2,1)S(1)}, u32[]{:S(2)}) copy-start(bf16[32,4096]{1,0:T(8,128)(2,1)S(1)} %collective-permute-done.297.refs_9_) | copy-start | bytes 786436
  46.2 9.3 %collective-permute-start.300 = (bf16[32,4096]{1,0:T(8,128)(2,1)}, bf16[32,4096]{1,0:T(8,128)(2,1)S(1)}, u32[]{:S(2)}, u32[]{:S(2)}) collective-permute-start(bf16[32,4096]{1,0:T(8,128)(2,1)} %get-tuple-element.937), channel_id=1, source_target_pairs={{0,3},{1,5},{2,7},{8,11},{9,13},{10,15},{16,19},{17,21},{18,23},{2... | collective-permute-start | bytes 786440 | tf_op jit(solution)/shard_map/ppermute | solution.py:528
  47.5 8.0 %copy-start.9 = (bf16[32,4096]{1,0:T(8,128)(2,1)}, bf16[32,4096]{1,0:T(8,128)(2,1)S(1)}, u32[]{:S(2)}) copy-start(bf16[32,4096]{1,0:T(8,128)(2,1)S(1)} %collective-permute-done.298.refs_10_) | copy-start | bytes 786436
  47.6 8.0 %copy-start.3 = (bf16[2,96,1024]{2,1,0:T(8,128)(2,1)}, bf16[2,96,1024]{2,1,0:T(8,128)(2,1)S(1)}, u32[]{:S(2)}) copy-start(bf16[2,96,1024]{2,1,0:T(8,128)(2,1)S(1)} %collective-permute-done.292.refs_4_) | copy-start | bytes 1179652
  52.7 2.9 %copy-start.10 = (bf16[32,4096]{1,0:T(8,128)(2,1)}, bf16[32,4096]{1,0:T(8,128)(2,1)S(1)}, u32[]{:S(2)}) copy-start(bf16[32,4096]{1,0:T(8,128)(2,1)S(1)} %collective-permute-done.299.refs_11_) | copy-start | bytes 786436
  55.5 0.7 copy-start.11
  55.5 0.9 copy-start.4
  69.2 8.9 %collective-permute-start.79 = (bf16[2,192,1024]{2,1,0:T(8,128)(2,1)S(1)}, bf16[2,192,1024]{2,1,0:T(8,128)(2,1)}, u32[]{:S(2)}, u32[]{:S(2)}) collective-permute-start(bf16[2,192,1024]{2,1,0:T(8,128)(2,1)S(1)} %get-tuple-element.655), channel_id=1, source_target_pairs={{0,1},{1,0},{2,3},{3,2},{4,5},{5,4},{6,7},{7,6},{8,9},{9,8},{10,11... | collective-permute-start | bytes 2359304 | tf_op jit(solution)/shard_map/cond/branch_10_fun/ppermute | solution.py:468
  69.3 8.8 %collective-permute-start.80 = (bf16[2,64,1024]{2,1,0:T(8,128)(2,1)S(1)}, bf16[2,64,1024]{2,1,0:T(8,128)(2,1)}, u32[]{:S(2)}, u32[]{:S(2)}) collective-permute-start(bf16[2,64,1024]{2,1,0:T(8,128)(2,1)S(1)} %get-tuple-element.656), channel_id=1, source_target_pairs={{1,0},{2,1},{3,2},{4,3},{5,4},{6,5},{7,6},{9,8},{10,9},{11,10},{12... | collective-permute-start | bytes 786440 | tf_op jit(solution)/shard_map/cond/branch_10_fun/ppermute | solution.py:468
  70.6 7.5 %collective-permute-start.78 = (bf16[16,4096]{1,0:T(8,128)(2,1)}, bf16[16,4096]{1,0:T(8,128)(2,1)}, u32[]{:S(2)}, u32[]{:S(2)}) collective-permute-start(bf16[16,4096]{1,0:T(8,128)(2,1)} %get-tuple-element.654), channel_id=1, source_target_pairs={{0,8},{8,24},{16,0},{24,16},{1,9},{9,25},{17,1},{25,17},{2,10},{10... | collective-permute-start | bytes 393224 | tf_op jit(solution)/shard_map/cond/branch_10_fun/ppermute | solution.py:477
  78.0 2.2 %copy-start.12 = (bf16[16,4096]{1,0:T(8,128)(2,1)S(1)}, bf16[16,4096]{1,0:T(8,128)(2,1)}, u32[]{:S(2)}) copy-start(bf16[16,4096]{1,0:T(8,128)(2,1)} %get-tuple-element.947) | copy-start | bytes 393220
  80.2 13.4 %collective-permute-start.161 = (bf16[2,64,1024]{2,1,0:T(8,128)(2,1)S(1)}, bf16[2,64,1024]{2,1,0:T(8,128)(2,1)}, u32[]{:S(2)}, u32[]{:S(2)}) collective-permute-start(bf16[2,64,1024]{2,1,0:T(8,128)(2,1)S(1)} %get-tuple-element.737), channel_id=1, source_target_pairs={{0,2},{1,3},{2,0},{3,1},{4,6},{5,7},{6,4},{7,5},{8,10},{9,11},{10,... | collective-permute-start | bytes 786440 | tf_op jit(solution)/shard_map/cond/branch_10_fun/ppermute | solution.py:468
  82.8 11.0 %collective-permute-start.162 = (bf16[2,64,1024]{2,1,0:T(8,128)(2,1)S(1)}, bf16[2,64,1024]{2,1,0:T(8,128)(2,1)}, u32[]{:S(2)}, u32[]{:S(2)}) collective-permute-start(bf16[2,64,1024]{2,1,0:T(8,128)(2,1)S(1)} %get-tuple-element.738), channel_id=1, source_target_pairs={{0,4},{1,5},{2,6},{3,7},{4,0},{5,1},{6,2},{7,3},{8,12},{9,13},{10,... | collective-permute-start | bytes 786440 | tf_op jit(solution)/shard_map/cond/branch_10_fun/ppermute | solution.py:468
  84.6 6.0 %collective-permute-start.160 = (bf16[16,4096]{1,0:T(8,128)(2,1)S(1)}, bf16[16,4096]{1,0:T(8,128)(2,1)}, u32[]{:S(2)}, u32[]{:S(2)}) collective-permute-start(bf16[16,4096]{1,0:T(8,128)(2,1)S(1)} %get-tuple-element.736), channel_id=1, source_target_pairs={{0,8},{8,24},{16,0},{24,16},{1,9},{9,25},{17,1},{25,17},{2,10},{10... | collective-permute-start | bytes 393224 | tf_op jit(solution)/shard_map/cond/branch_10_fun/ppermute | solution.py:477
  85.4 8.2 %collective-permute-start.163 = (bf16[2,32,1024]{2,1,0:T(8,128)(2,1)S(1)}, bf16[2,32,1024]{2,1,0:T(8,128)(2,1)}, u32[]{:S(2)}, u32[]{:S(2)}) collective-permute-start(bf16[2,32,1024]{2,1,0:T(8,128)(2,1)S(1)} %get-tuple-element.739), channel_id=1, source_target_pairs={{0,6},{1,7},{2,4},{3,5},{4,2},{5,3},{6,0},{7,1},{8,14},{9,15},{10,... | collective-permute-start | bytes 393224 | tf_op jit(solution)/shard_map/cond/branch_10_fun/ppermute | solution.py:468
  95.3 6.0 %collective-permute-start.246 = (bf16[2,32,1024]{2,1,0:T(8,128)(2,1)S(1)}, bf16[2,32,1024]{2,1,0:T(8,128)(2,1)}, u32[]{:S(2)}, u32[]{:S(2)}) collective-permute-start(bf16[2,32,1024]{2,1,0:T(8,128)(2,1)S(1)} %get-tuple-element.822), channel_id=1, source_target_pairs={{0,8},{8,24},{16,0},{24,16},{1,9},{9,25},{17,1},{25,17},{2,10},{10... | collective-permute-start | bytes 393224 | tf_op jit(solution)/shard_map/cond/branch_10_fun/ppermute | solution.py:477
  96.4 5.1 %collective-permute-start.247 = (bf16[64,1024]{1,0:T(8,128)(2,1)S(1)}, bf16[64,1024]{1,0:T(8,128)(2,1)}, u32[]{:S(2)}, u32[]{:S(2)}) collective-permute-start(bf16[64,1024]{1,0:T(8,128)(2,1)S(1)} %get-tuple-element.823), channel_id=1, source_target_pairs={{0,2},{1,3},{2,0},{3,1},{4,6},{5,7},{6,4},{7,5},{8,10},{9,11},{10,... | collective-permute-start | bytes 393224 | tf_op jit(solution)/shard_map/cond/branch_10_fun/ppermute | solution.py:468
  97.9 5.1 %collective-permute-start.248 = (bf16[64,1024]{1,0:T(8,128)(2,1)S(1)}, bf16[64,1024]{1,0:T(8,128)(2,1)}, u32[]{:S(2)}, u32[]{:S(2)}) collective-permute-start(bf16[64,1024]{1,0:T(8,128)(2,1)S(1)} %get-tuple-element.824), channel_id=1, source_target_pairs={{0,4},{1,5},{2,6},{3,7},{4,0},{5,1},{6,2},{7,3},{8,12},{9,13},{10,... | collective-permute-start | bytes 393224 | tf_op jit(solution)/shard_map/cond/branch_10_fun/ppermute | solution.py:468
Sparse Core Ops, SparseCore 0:
  10.1 30.6 all-gather.2
where the time goes:
time: 113 us; the launch traced here: 112 us
  waiting for transfers between devices  37.6 us (33%)
  starting transfers between devices  30.5 us (27%)
  Pallas kernels  26.5 us (23%)
  between operations  15 us (13%)
  local copies, waits for them, and re-layouts  2.42 us (2%)
    ppermute x4, waiting for transfers between devices, branch(): lax.ppermute(rows, 'rollout', pairs)  16.3 us
    pallas_call x1, Pallas kernels, attend(): pl.pallas_call(functools.partial(attend_kernel, VIS // len(blocks), len(b...  12.7 us
    ppermute x8, starting transfers between devices, move_beside(): lax.ppermute(array, 'ctx', pairs)  10.8 us
    ppermute x4, waiting for transfers between devices, image_windows(): lax.ppermute(rows, 'ctx', pairs)  7.96 us
    ppermute x8, waiting for transfers between devices, xor_permute(): return lax.ppermute(rows, 'ctx', xor_pairs(step))  7.17 us
    ppermute x8, starting transfers between devices, xor_permute(): return lax.ppermute(rows, 'ctx', xor_pairs(step))  6.99 us
    ppermute x4, starting transfers between devices, branch(): lax.ppermute(rows, 'rollout', pairs)  6.17 us
    ppermute x8, waiting for transfers between devices, move_beside(): lax.ppermute(array, 'ctx', pairs)  6.16 us
  transfers between devices with their start and end apart: 26, of which 13 were waited for; matrix products, arithmetic and copies ran while one was open for 0% of the time, Pallas kernels for 5%

commit v1 on v0

--- a/solution.py
+++ b/solution.py
@@ -46,7 +46,7 @@
     )
 
 
-def first_kernel(halo, seq_ref, vis_ref, image_ref, kv_ref, number_ref, *out_refs):
+def send_first(halo, seq_ref, vis_ref, image_ref, kv_ref, number_ref, *out_refs):
     ikv_ref, iq_ref, text_ref, tail_ref = out_refs
     groups = seq_ref.shape[0]
     group = lax.axis_index("rollout")
@@ -80,25 +80,6 @@
         tail_ref[part] = kv_ref[0, part, tok_rows - halo :]
 
 
-def first_arrays(seq_image, vis_start, image_rows, keys_values, halo):
-    rows = image_rows.shape[1]
-    smem = pl.BlockSpec(memory_space=pltpu.SMEM)
-    vmem = pl.BlockSpec(memory_space=pltpu.VMEM)
-    tail = min(halo, keys_values.shape[2])
-    return pl.pallas_call(
-        functools.partial(first_kernel, tail),
-        in_specs=[smem, smem, vmem, vmem],
-        out_specs=[smem, vmem, vmem, vmem, vmem],
-        out_shape=[
-            jax.ShapeDtypeStruct((3,), jnp.int32),
-            jax.ShapeDtypeStruct((2, rows, KV_WIDTH), jnp.bfloat16),
-            jax.ShapeDtypeStruct((rows, Q_WIDTH), jnp.bfloat16),
-            jax.ShapeDtypeStruct((2, PROMPT, KV_WIDTH), jnp.bfloat16),
-            jax.ShapeDtypeStruct((2, tail, KV_WIDTH), jnp.bfloat16),
-        ],
-    )(seq_image, vis_start, image_rows, keys_values)
-
-
 def segments(positions, length_ref):
     end = jnp.int32(PREFIX)
     segment = jnp.where(positions < PREFIX, 0, 1)
@@ -112,36 +93,24 @@
     return jnp.where(visible, 0.0, HIDDEN)
 
 
-def second_kernel(
-    targets, tok_rows, image_rows, halo, vis_ref, length_ref, d_ref, kv_ref, t_ref, r_ref, *out_refs
-):
-    *window_refs, near_ref, whole_ref, image_ref, text_ref = out_refs
+def first_kernel(halo, tail, seq_ref, vis_ref, length_ref, *refs):
+    image_in_ref, kv_ref, d_ref, *out_refs = refs
+    first_refs, window_ref, mask_refs = out_refs[:5], out_refs[5], out_refs[6:]
+    near_ref, whole_ref, image_ref = mask_refs
     here = lax.axis_index("ctx")
     ctx_size = lax.axis_size("ctx")
-    row = lax.broadcasted_iota(jnp.int32, (IMAGE_BLOCK, tok_rows), 0)
-    column = lax.broadcasted_iota(jnp.int32, (IMAGE_BLOCK, tok_rows), 1)
-    place = jnp.where(row < image_rows, row, 1 << 20)
-    picks = []
-    for blocks in targets:
-        for default, special in blocks:
-            target = here if default is None else default
-            for source, other in special:
-                target = jnp.where(here == source, other, target)
-            begin = vis_ref[0] + image_rows * target - tok_rows * here
-            picks.append(jnp.where(column == place + begin, 1.0, 0.0).astype(jnp.bfloat16))
-    picked = dot_nn(jnp.concatenate(picks, axis=0), d_ref[...]).astype(jnp.bfloat16)
-    at = 0
-    for window_ref in window_refs:
-        window_ref[...] = picked[at : at + window_ref.shape[0]]
-        at += window_ref.shape[0]
+    tok_rows = d_ref.shape[0]
+    image_rows = image_in_ref.shape[1]
+    row = lax.broadcasted_iota(jnp.int32, (VIS, tok_rows), 0)
+    column = lax.broadcasted_iota(jnp.int32, (VIS, tok_rows), 1)
+    pick = column == row + (vis_ref[0] - tok_rows * here)
+    pick = jnp.where(pick, 1.0, 0.0).astype(jnp.bfloat16)
+    window_ref[...] = dot_nn(pick, d_ref[...]).astype(jnp.bfloat16)
 
     @pl.when(pl.program_id(0) == 0)
     def _():
+        send_first(tail, seq_ref, vis_ref, image_in_ref, kv_ref, *first_refs)
         vis = vis_ref[0]
-        text = t_ref[...].astype(jnp.float32) + r_ref[...].astype(jnp.float32)
-        if kv_ref.shape[1] == IMAGE_BLOCK:
-            text_ref[:, :IMAGE_BLOCK] = kv_ref[...]
-        text_ref[:, text_ref.shape[1] - PROMPT :] = text.astype(jnp.bfloat16)
         own_at = lax.broadcasted_iota(jnp.int32, (8, tok_rows), 1) + here * tok_rows
         own_segment = segments(own_at, length_ref)[:1]
         placeholder = (own_at >= vis) & (own_at < vis + VIS)
@@ -169,45 +138,48 @@
         image_ref[VIS:] = hide(text_at <= image_row)
 
 
-def second_arrays(vis_start, lengths, cotangent, image_kv, text, received, halo):
+def first_arrays(seq_image, vis_start, lengths, image_rows, keys_values, cotangent, halo):
+    rows = image_rows.shape[1]
     tok_rows, width = cotangent.shape
-    image_rows = image_kv.shape[1]
-    text_rows = PROMPT + (image_rows if image_rows == IMAGE_BLOCK else 0)
-    targets, rounds = window_targets(lax.axis_size("ctx"), tok_rows, image_rows)
-    counts = [len(blocks) * IMAGE_BLOCK for blocks in targets]
+    tail = min(halo, tok_rows)
     block = 2048
     spec = pl.BlockSpec
     smem = spec(memory_space=pltpu.SMEM)
     lanes = RATIO * IMAGE_BLOCK
     near = PROMPT + halo + tok_rows
     whole = lambda *shape: spec(shape, lambda at: (0,) * len(shape))
-    out = pl.pallas_call(
-        functools.partial(second_kernel, targets, tok_rows, image_rows, halo),
+    kept = [
+        ((2, rows, KV_WIDTH), jnp.bfloat16),
+        ((rows, Q_WIDTH), jnp.bfloat16),
+        ((2, PROMPT, KV_WIDTH), jnp.bfloat16),
+        ((2, tail, KV_WIDTH), jnp.bfloat16),
+    ]
+    masks = [
+        ((near, tok_rows), jnp.float32),
+        ((8, tok_rows), jnp.float32),
+        ((PREFIX, lanes), jnp.float32),
+    ]
+    number, *out = pl.pallas_call(
+        functools.partial(first_kernel, halo, tail),
         grid=(width // block,),
         in_specs=[
             smem,
             smem,
+            smem,
+            whole(*image_rows.shape),
+            whole(*keys_values.shape),
             spec((tok_rows, block), lambda at: (0, at)),
-            whole(2, image_rows, KV_WIDTH),
-            whole(2, PROMPT, KV_WIDTH),
-            whole(2, PROMPT, KV_WIDTH),
         ],
-        out_specs=[spec((count, block), lambda at: (0, at)) for count in counts]
-        + [
-            whole(near, tok_rows),
-            whole(8, tok_rows),
-            whole(PREFIX, lanes),
-            whole(2, text_rows, KV_WIDTH),
-        ],
-        out_shape=[jax.ShapeDtypeStruct((count, width), jnp.bfloat16) for count in counts]
-        + [
-            jax.ShapeDtypeStruct((near, tok_rows), jnp.float32),
-            jax.ShapeDtypeStruct((8, tok_rows), jnp.float32),
-            jax.ShapeDtypeStruct((PREFIX, lanes), jnp.float32),
-            jax.ShapeDtypeStruct((2, text_rows, KV_WIDTH), jnp.bfloat16),
-        ],
-    )(vis_start, lengths, cotangent, image_kv, text, received)
-    return out[: len(counts)], rounds, out[len(counts) :]
+        out_specs=[smem]
+        + [whole(*shape) for shape, _ in kept]
+        + [spec((VIS, block), lambda at: (0, at))]
+        + [whole(*shape) for shape, _ in masks],
+        out_shape=[jax.ShapeDtypeStruct((3,), jnp.int32)]
+        + [jax.ShapeDtypeStruct(*pair) for pair in kept]
+        + [jax.ShapeDtypeStruct((VIS, width), jnp.bfloat16)]
+        + [jax.ShapeDtypeStruct(*pair) for pair in masks],
+    )(seq_image, vis_start, lengths, image_rows, keys_values, cotangent)
+    return number, out[:4], out[4], out[5:]
 
 
 def first_products(parts, q_rows, d_rows):
@@ -387,6 +359,7 @@
 ):
     heads = 2
     near_bias, whole_bias, image_bias = masks
+    sources = range(windows.shape[0] // IMAGE_BLOCK)[: (VIS + PROMPT - 1) // queries.shape[0] + 1]
     own = queries.shape[0]
     halo = halo_kv.shape[1]
     groups = every_q.shape[0]
@@ -402,7 +375,7 @@
             VIS // len(blocks),
             len(blocks),
             len(texts),
-            len(windows),
+            len(sources),
             heads,
             halo,
             own,
@@ -420,7 +393,10 @@
             spec((1, 2, own, heads * HEAD_DIM), lambda at: (0, 0, 0, at)),
         ]
         + [kv_spec(block.shape[1]) for block in [*blocks, *texts]]
-        + [q_spec(IMAGE_BLOCK) for _ in windows],
+        + [
+            spec((IMAGE_BLOCK, heads * GROUP_WIDTH), lambda at, source=source: (source, at))
+            for source in sources
+        ],
         out_specs=[
             q_spec(own),
             q_spec(IMAGE_HALF),
@@ -456,7 +432,7 @@
         own_kv,
         *blocks,
         *texts,
-        *windows,
+        *[windows for _ in sources],
     )
 
 
@@ -478,57 +454,6 @@
 
     orders = itertools.permutations(range(groups))
     return lax.switch(number[0], [branch(images) for images in orders], rows, arrays)
-
-
-def window_rounds(ctx_size, tok_rows, image_rows):
-    rounds = []
-    for target in range(ctx_size):
-        lowest = (image_rows * target + 1) // tok_rows
-        highest = (image_rows * target + image_rows - 1 + PROMPT - 1) // tok_rows
-        for source in range(lowest, highest + 1):
-            if source == target:
-                continue
-            for pairs in rounds:
-                if all(s != source and t != target for s, t in pairs):
-                    pairs.append((source, target))
-                    break
-            else:
-                rounds.append([(source, target)])
-    return rounds
-
-
-def window_targets(ctx_size, tok_rows, image_rows):
-    rounds = window_rounds(ctx_size, tok_rows, image_rows)
-    if ctx_size != 8:
-        return [[(None, [])]] + [[(None, pairs)] for pairs in rounds], rounds
-    rounds = [[(0, 2), (1, 4), (2, 6)], [(0, 3), (1, 5), (2, 7)], [(1, 6)], [(1, 7)]]
-    swapped = [(2, [(0, 1)]), (3, [])]
-    return [[(None, [])]] + [[(None, pairs)] for pairs in rounds] + [swapped], rounds
-
-
-def join_windows(own, one, two, swapped):
-    here = lax.axis_index("ctx")
-    wide = lambda rows: rows.astype(jnp.float32)
-    near, far = swapped[:IMAGE_BLOCK], swapped[IMAGE_BLOCK:]
-    sums = [
-        jnp.where(here == 1, wide(own) + wide(near), wide(own)),
-        jnp.where(here == 0, wide(one) + wide(near), wide(one)),
-        jnp.where(here == 0, wide(two) + wide(far), wide(two)),
-    ]
-    return [part.astype(jnp.bfloat16) for part in sums]
-
-
-def image_windows(windows, rounds):
-    own, *sent = windows
-    if lax.axis_size("ctx") == 8:
-        one, two, three, four, swapped = sent
-        late = [lax.ppermute(rows, "ctx", pairs) for rows, pairs in zip((three, four), rounds[2:])]
-        own, one, two = on_device(join_windows, own, one, two, xor_permute(swapped, 1))
-        return [own] + late + [
-            lax.ppermute(rows, "ctx", pairs) for rows, pairs in zip((one, two), rounds)
-        ]
-    parts = [own] + [lax.ppermute(rows, "ctx", pairs) for rows, pairs in zip(sent, rounds)]
-    return [sum(part.astype(jnp.float32) for part in parts).astype(jnp.bfloat16)]
 
 
 def xor_pairs(step):
@@ -573,17 +498,26 @@
     return list(range(2, ctx_size, 2))
 
 
-def gather_prefix(image_kv, text, late_shard):
+def join_text(image_kv, text, received):
+    return [jnp.concatenate([image_kv, add_text(text, received)], axis=1)]
+
+
+def add_text(text, received):
+    return (text.astype(jnp.float32) + received.astype(jnp.float32)).astype(jnp.bfloat16)
+
+
+def gather_prefix(image_kv, text, received, late_shard):
     ctx_size = lax.axis_size("ctx")
     steps = chip_steps(ctx_size)
     if ctx_size == 8:
+        (text,) = on_device(join_text, image_kv, text, received)
         mine = [text, xor_permute(image_kv, 2), xor_permute(text, 4), xor_permute(image_kv, 6)]
         blocks = mine + [xor_permute(block, 1) for block in mine]
         return blocks, [blocks[at] for at in (0, 2, 4, 6)]
     mine = jnp.concatenate(
         [image_kv] + [xor_permute(image_kv, step) for step in steps], axis=1
     )
-    return [mine, xor_permute(mine, 1)], list(spread_text(text, late_shard))
+    return [mine, xor_permute(mine, 1)], list(spread_text(add_text(text, received), late_shard))
 
 
 def split_sums(image_rows, steps, d_mine, d_pair, other):
@@ -719,17 +653,17 @@
     halo = -(-(longest - 1) // 64) * 64
     q_own, d_own = queries[0], cotangent[0]
 
-    number, image_kv, image_q, text, tail = first_arrays(
-        seq_image, vis_start, image_rows, keys_values, halo
-    )
+    number, (image_kv, image_q, text, tail), windows, masks = first_arrays(
+        seq_image, vis_start, comp_lengths, image_rows, keys_values, d_own, halo
+    )
+    windows = lax.all_to_all(windows, "ctx", split_axis=0, concat_axis=0, tiled=True)
+    if image_count < IMAGE_BLOCK:
+        windows = windows.reshape(ctx_size, image_count, -1)[: (VIS + PROMPT - 1) // tok_rows + 1]
+        windows = jnp.sum(windows.astype(jnp.float32), axis=0).astype(jnp.bfloat16)
+        windows = jnp.pad(windows, ((0, IMAGE_BLOCK - image_count), (0, 0)))
     every_q = gather_queries(image_q)
-    image_kv, swapped = route(image_kv, number, False, [(text, xor_pairs(late_shard))])
-    image_kv, d_later = lax.optimization_barrier((image_kv, d_own))
-    windows, rounds, (*masks, text) = second_arrays(
-        vis_start, comp_lengths, d_later, image_kv, text, swapped, halo
-    )
-    blocks, texts = gather_prefix(image_kv, text, late_shard)
-    windows = image_windows(windows, rounds)
+    image_kv, received = route(image_kv, number, False, [(text, xor_pairs(late_shard))])
+    blocks, texts = gather_prefix(image_kv, text, received, late_shard)
     halo_kv = halo_rows(tail, halo, tok_rows)
 
     grad_q, *d_image_q, d_mine, d_pair, d_halo, d_own_kv = attend(

time: 113 us -> 132 us (1.17)
  waiting for transfers between devices: 37.6 us -> 59.8 us
  Pallas kernels: 26.5 us -> 24.3 us
    ppermute x8, waiting for transfers between devices: 6.16 us -> 24.9 us  [move_beside(): lax.ppermute(array, 'ctx', pairs)]
    ppermute x8 -> x7, waiting for transfers between devices: 7.17 us -> 16.2 us  [xor_permute(): return lax.ppermute(rows, 'ctx', xor_pairs(step))]
    ppermute x4 -> x0, waiting for transfers between devices: 7.96 us -> none  [image_windows(): lax.ppermute(rows, 'ctx', pairs)]
    all_to_all x0 -> x1, starting transfers between devices: none -> 5.18 us  [per_device(): lax.all_to_all(windows, 'ctx', split_axis=0, concat_axis=0, tiled=True)]
    ppermute x4, starting transfers between devices: 6.17 us -> 10.7 us  [branch(): lax.ppermute(rows, 'rollout', pairs)]
    ppermute x4 -> x0, starting transfers between devices: 4.13 us -> none  [image_windows(): lax.ppermute(rows, 'ctx', pairs)]
    ppermute x8 -> x7, starting transfers between devices: 6.99 us -> 4.41 us  [xor_permute(): return lax.ppermute(rows, 'ctx', xor_pairs(step))]
    ppermute x8, starting transfers between devices: 10.8 us -> 8.71 us  [move_beside(): lax.ppermute(array, 'ctx', pairs)]
  transfers between devices with their start and end apart: 26 -> 22, of which waited for: 13 -> 12; matrix products, arithmetic and copies ran while one was open for 0% -> 0% of each run, Pallas kernels for 5% -> 1%
where the time goes in v1:
time: 132 us
  waiting for transfers between devices  59.8 us (45%)
  starting transfers between devices  30.8 us (23%)
  Pallas kernels  24.3 us (18%)
  between operations  14.8 us (11%)
  local copies, waits for them, and re-layouts  2.21 us (2%)
    ppermute x8, waiting for transfers between devices, move_beside(): lax.ppermute(array, 'ctx', pairs)  24.9 us
    ppermute x4, waiting for transfers between devices, branch(): lax.ppermute(rows, 'rollout', pairs)  18.1 us
    ppermute x7, waiting for transfers between devices, xor_permute(): return lax.ppermute(rows, 'ctx', xor_pairs(step))  16.2 us
    pallas_call x1, Pallas kernels, attend(): pl.pallas_call(functools.partial(attend_kernel, VIS // len(blocks), len(b...  12.7 us
    ppermute x4, starting transfers between devices, branch(): lax.ppermute(rows, 'rollout', pairs)  10.7 us
    ppermute x8, starting transfers between devices, move_beside(): lax.ppermute(array, 'ctx', pairs)  8.71 us
    pallas_call x3, Pallas kernels, on_device(): pl.pallas_call(kernel, grid=(2,), in_specs=[spec(array) for array in arra...  5.39 us
    all_to_all x1, starting transfers between devices, per_device(): lax.all_to_all(windows, 'ctx', split_axis=0, concat_axis=0, tiled=True)  5.18 us
  transfers between devices with their start and end apart: 22, of which 12 were waited for; matrix products, arithmetic and copies ran while one was open for 0% of the time, Pallas kernels for 1%

profile of v1, /device:TPU:0, one launch (start us, length us, event | category | flops | bytes accessed | tf_op | source)
XLA Modules:
  0.0 132.2 jit_solution(7405698634227221735)
XLA Ops:
  7.8 3.8 %shard_map.94 = (s32[3]{0:T(128)}, bf16[2,32,1024]{2,1,0:T(8,128)(2,1)S(1)}, bf16[32,4096]{1,0:T(8,128)(2,1)}, bf16[2,64,1024]{2,1,0:T(8,128)(2,1)S(1)}, bf16[2,...) custom-call(s32[4]{0:T(128)} %seq_ref.1, ...), custom_call_target="tpu_custom_call" | custom-call | tf_op jit(solution)/shard_map/pallas_call | solution.py:162
  11.7 5.2 %all-to-all-start = ((bf16[8,32,4096]{2,1,0:T(8,128)(2,1)}), bf16[8,32,4096]{2,1,0:T(8,128)(2,1)S(1)}, u32[]{:S(2)}, u32[]{:S(2)}) async-start(bf16[8,32,4096]{2,1,0:T(8,128)(2,1)} %bitcast.13), calls=%async_computation | async-start | bytes 4194304 | tf_op jit(solution)/shard_map/all_to_all | solution.py:659
  16.8 0.0 all-gather.3.cloned.1.call-start
  16.9 0.7 all-gather.3.cloned.1.call-update
  17.6 30.7 %conditional.4 = (bf16[2,32,1024]{2,1,0:T(8,128)(2,1)}, bf16[2,64,1024]{2,1,0:T(8,128)(2,1)}) conditional(s32[]{:T(128)} %bitcast.3, (bf16[2,32,1024]{2,1,0:T(8,128)(2,1)S(1)}, bf16[2,64,1024]{2,1,0:T(8,128)(2,1)S(1)}) %tuple.368, (bf16[2,32,1024]{2,1,0:T(8,128)(2,1)S(1)}, ...), branch_computations={%region_0.0_spmd, %region_1.0_spmd, %region_2.0_spmd, %region_3.0_... | conditional | bytes 1572960 | solution.py:456
  17.7 2.1 %collective-permute-start.45 = (bf16[2,64,1024]{2,1,0:T(8,128)(2,1)S(1)}, bf16[2,64,1024]{2,1,0:T(8,128)(2,1)}, u32[]{:S(2)}, u32[]{:S(2)}) collective-permute-start(bf16[2,64,1024]{2,1,0:T(8,128)(2,1)S(1)} %get-tuple-element.621), channel_id=1, source_target_pairs={{0,2},{1,3},{2,0},{3,1},{4,6},{5,7},{6,4},{7,5},{8,10},{9,11},{10,... | collective-permute-start | bytes 786440 | tf_op jit(solution)/shard_map/cond/branch_22_fun/ppermute | solution.py:444
  19.7 2.6 %collective-permute-start.44 = (bf16[2,32,1024]{2,1,0:T(8,128)(2,1)S(1)}, bf16[2,32,1024]{2,1,0:T(8,128)(2,1)}, u32[]{:S(2)}, u32[]{:S(2)}) collective-permute-start(bf16[2,32,1024]{2,1,0:T(8,128)(2,1)S(1)} %get-tuple-element.620), channel_id=1, source_target_pairs={{24,0},{16,8},{0,16},{8,24},{25,1},{17,9},{1,17},{9,25},{26,2},{18... | collective-permute-start | bytes 393224 | tf_op jit(solution)/shard_map/cond/branch_22_fun/ppermute | solution.py:453
  22.3 4.8 %collective-permute-done.44 = bf16[2,32,1024]{2,1,0:T(8,128)(2,1)} collective-permute-done((bf16[2,32,1024]{2,1,0:T(8,128)(2,1)S(1)}, bf16[2,32,1024]{2,1,0:T(8,128)(2,1)}, u32[]{:S(2)}, u32[]{:S(2)}) %collective-permute-start.44) | collective-permute-done | bytes 131104 | tf_op jit(solution)/shard_map/cond/branch_22_fun/ppermute | solution.py:453
  27.1 21.2 %collective-permute-done.45 = bf16[2,64,1024]{2,1,0:T(8,128)(2,1)} collective-permute-done((bf16[2,64,1024]{2,1,0:T(8,128)(2,1)S(1)}, bf16[2,64,1024]{2,1,0:T(8,128)(2,1)}, u32[]{:S(2)}, u32[]{:S(2)}) %collective-permute-start.45) | collective-permute-done | bytes 262176 | tf_op jit(solution)/shard_map/cond/branch_22_fun/ppermute | solution.py:444
  48.3 1.8 %shard_map.95.refs_0_ = bf16[2,96,1024]{2,1,0:T(8,128)(2,1)} custom-call(bf16[2,32,1024]{2,1,0:T(8,128)(2,1)} %get-tuple-element.913.refs_0_, bf16[2,64,1024]{2,1,0:T(8,128)(2,1)S(1)} %get-tuple-element.912.refs_1_, bf16[2,64,1024]{2,1,0:T(8,128)(2,1)} %get-tuple-element.914.refs_2_), custom_call_target="tpu_custom_call" | custom-call | flops 1 | bytes 1 | tf_op jit(solution)/shard_map/pallas_call | solution.py:482
  50.1 1.5 %collective-permute-start.290 = (bf16[2,96,1024]{2,1,0:T(8,128)(2,1)}, bf16[2,96,1024]{2,1,0:T(8,128)(2,1)S(1)}, u32[]{:S(2)}, u32[]{:S(2)}) collective-permute-start(bf16[2,96,1024]{2,1,0:T(8,128)(2,1)} %shard_map.95.refs_0_), channel_id=1, source_target_pairs={{0,4},{1,5},{2,6},{3,7},{4,0},{5,1},{6,2},{7,3},{8,12},{9,13},{10,... | collective-permute-start | bytes 1179656 | tf_op jit(solution)/shard_map/ppermute | solution.py:464
  51.5 0.0 collective-permute-start.292
  51.5 9.4 %collective-permute-done.290.refs_2_ = bf16[2,96,1024]{2,1,0:T(8,128)(2,1)S(1)} collective-permute-done((bf16[2,96,1024]{2,1,0:T(8,128)(2,1)}, bf16[2,96,1024]{2,1,0:T(8,128)(2,1)S(1)}, u32[]{:S(2)}, u32[]{:S(2)}) %collective-permute-start.290) | collective-permute-done | bytes 393248 | tf_op jit(solution)/shard_map/ppermute | solution.py:464
  60.9 1.5 %collective-permute-start.291 = (bf16[2,32,1024]{2,1,0:T(8,128)(2,1)}, bf16[2,32,1024]{2,1,0:T(8,128)(2,1)S(1)}, u32[]{:S(2)}, u32[]{:S(2)}) collective-permute-start(bf16[2,32,1024]{2,1,0:T(8,128)(2,1)} %get-tuple-element.913.refs_0_), channel_id=1, source_target_pairs={{0,6},{1,7},{2,4},{3,5},{4,2},{5,3},{6,0},{7,1},{8,14},{9,15},{10,... | collective-permute-start | bytes 393224 | tf_op jit(solution)/shard_map/ppermute | solution.py:464
  62.4 1.4 %collective-permute-start.289 = (bf16[2,32,1024]{2,1,0:T(8,128)(2,1)}, bf16[2,32,1024]{2,1,0:T(8,128)(2,1)S(1)}, u32[]{:S(2)}, u32[]{:S(2)}) collective-permute-start(bf16[2,32,1024]{2,1,0:T(8,128)(2,1)} %get-tuple-element.913.refs_0_), channel_id=1, source_target_pairs={{0,2},{1,3},{2,0},{3,1},{4,6},{5,7},{6,4},{7,5},{8,10},{9,11},{10,... | collective-permute-start | bytes 393224 | tf_op jit(solution)/shard_map/ppermute | solution.py:464
  63.9 1.9 %collective-permute-start.288 = (bf16[2,64,1024]{2,1,0:T(8,128)(2,1)}, bf16[2,64,1024]{2,1,0:T(8,128)(2,1)S(1)}, u32[]{:S(2)}, u32[]{:S(2)}) collective-permute-start(bf16[2,64,1024]{2,1,0:T(8,128)(2,1)} %get-tuple-element.910), channel_id=1, source_target_pairs={{0,1},{1,2},{2,3},{3,4},{4,5},{5,6},{6,7},{8,9},{9,10},{10,11},{11... | collective-permute-start | bytes 786440 | tf_op jit(solution)/shard_map/ppermute | solution.py:577
  65.7 2.6 %collective-permute-done.291.refs_3_ = bf16[2,32,1024]{2,1,0:T(8,128)(2,1)S(1)} collective-permute-done((bf16[2,32,1024]{2,1,0:T(8,128)(2,1)}, bf16[2,32,1024]{2,1,0:T(8,128)(2,1)S(1)}, u32[]{:S(2)}, u32[]{:S(2)}) %collective-permute-start.291) | collective-permute-done | bytes 131104 | tf_op jit(solution)/shard_map/ppermute | solution.py:464
  68.3 0.0 collective-permute-start.295
  68.3 2.8 %collective-permute-done.289.refs_1_ = bf16[2,32,1024]{2,1,0:T(8,128)(2,1)S(1)} collective-permute-done((bf16[2,32,1024]{2,1,0:T(8,128)(2,1)}, bf16[2,32,1024]{2,1,0:T(8,128)(2,1)S(1)}, u32[]{:S(2)}, u32[]{:S(2)}) %collective-permute-start.289) | collective-permute-done | bytes 131104 | tf_op jit(solution)/shard_map/ppermute | solution.py:464
  71.2 1.3 %collective-permute-done.293.refs_5_ = bf16[2,32,1024]{2,1,0:T(8,128)(2,1)S(1)} collective-permute-done((bf16[2,32,1024]{2,1,0:T(8,128)(2,1)S(1)}, bf16[2,32,1024]{2,1,0:T(8,128)(2,1)S(1)}, u32[]{:S(2)}, u32[]{:S(2)}) %collective-permute-start.293) | collective-permute-done | bytes 131104 | tf_op jit(solution)/shard_map/ppermute | solution.py:464
  72.5 0.6 copy-done.8
  73.2 0.0 all-gather.3.cloned.1.call-done
  73.2 0.7 copy-done.2
  73.9 0.1 copy-done.3
  74.1 0.7 copy-done
  74.8 12.7 %shard_map.96 = (bf16[128,4096]{1,0:T(8,128)(2,1)}, bf16[16,4096]{1,0:T(8,128)(2,1)}, bf16[16,4096]{1,0:T(8,128)(2,1)}, bf16[2,128,1024]{2,1,0:T(8,128)(2,1)}, b...) custom-call(s32[3]{0:T(128)} %get-tuple-element.905.number_ref, ...), custom_call_target="tpu_custom_call" | custom-call | flops 3103784960 | bytes 12582912 | tf_op jit(solution)/shard_map/pallas_call | solution.py:372
  87.5 11.8 %conditional.5 = (bf16[16,4096]{1,0:T(8,128)(2,1)}, bf16[2,192,1024]{2,1,0:T(8,128)(2,1)}, bf16[2,64,1024]{2,1,0:T(8,128)(2,1)}) conditional(s32[]{:T(128)} %bitcast.3, (bf16[16,4096]{1,0:T(8,128)(2,1)}, bf16[2,192,1024]{2,1,0:T(8,128)(2,1)S(1)}, bf16[2,64,1024]{2,1,0:T(8,128)(2,1)}) %tuple.369, ...), branch_computations={%region_24.0_spmd, %region_25.0_spmd, %region_26.0_spmd, %region_2... | conditional | bytes 4718736 | solution.py:456
  87.5 0.2 collective-permute-start.115
  87.7 1.3 collective-permute-start.116
  89.0 3.7 %collective-permute-start.114 = (bf16[16,4096]{1,0:T(8,128)(2,1)}, bf16[16,4096]{1,0:T(8,128)(2,1)}, u32[]{:S(2)}, u32[]{:S(2)}) collective-permute-start(bf16[16,4096]{1,0:T(8,128)(2,1)} %get-tuple-element.690), channel_id=1, source_target_pairs={{0,24},{8,16},{16,0},{24,8},{1,25},{9,17},{17,1},{25,9},{2,26},{10... | collective-permute-start | bytes 393224 | tf_op jit(solution)/shard_map/cond/branch_22_fun/ppermute | solution.py:453
  92.7 6.6 %collective-permute-done.114 = bf16[16,4096]{1,0:T(8,128)(2,1)} collective-permute-done((bf16[16,4096]{1,0:T(8,128)(2,1)}, bf16[16,4096]{1,0:T(8,128)(2,1)}, u32[]{:S(2)}, u32[]{:S(2)}) %collective-permute-start.114) | collective-permute-done | bytes 131104 | tf_op jit(solution)/shard_map/cond/branch_22_fun/ppermute | solution.py:453
  99.3 2.1 %shard_map.97 = (f32[2,32,1024]{2,1,0:T(8,128)}, bf16[2,64,1024]{2,1,0:T(8,128)(2,1)S(1)}, bf16[2,64,1024]{2,1,0:T(8,128)(2,1)S(1)}, bf16[2,32,1024]{2,1,0:T(8,1...) custom-call(bf16[2,128,1024]{2,1,0:T(8,128)(2,1)} %get-tuple-element.917.refs_0_, ...), custom_call_target="tpu_custom_call" | custom-call | flops 1 | bytes 1 | tf_op jit(solution)/shard_map/pallas_call | solution.py:482
  101.5 11.7 %conditional.6 = (bf16[16,4096]{1,0:T(8,128)(2,1)}, bf16[2,64,1024]{2,1,0:T(8,128)(2,1)}, bf16[2,64,1024]{2,1,0:T(8,128)(2,1)}, bf16[2,32,1024]{2,1,0:T(8,128)(2,1)}) conditional(s32[]{:T(128)} %bitcast.3, (bf16[16,4096]{1,0:T(8,128)(2,1)S(1)}, bf16[2,64,1024]{2,1,0:T(8,128)(2,1)S(1)}, ...), branch_computations={%region_48.0_spmd, %region_49.0_spmd, %region_50.0_spmd, %region_5... | conditional | bytes 3145920 | solution.py:456
  101.5 1.3 %collective-permute-start.209 = (bf16[2,64,1024]{2,1,0:T(8,128)(2,1)S(1)}, bf16[2,64,1024]{2,1,0:T(8,128)(2,1)}, u32[]{:S(2)}, u32[]{:S(2)}) collective-permute-start(bf16[2,64,1024]{2,1,0:T(8,128)(2,1)S(1)} %get-tuple-element.785), channel_id=1, source_target_pairs={{0,2},{1,3},{2,0},{3,1},{4,6},{5,7},{6,4},{7,5},{8,10},{9,11},{10,... | collective-permute-start | bytes 786440 | tf_op jit(solution)/shard_map/cond/branch_22_fun/ppermute | solution.py:444
  102.8 1.3 collective-permute-start.210
  104.1 2.5 %collective-permute-start.208 = (bf16[16,4096]{1,0:T(8,128)(2,1)S(1)}, bf16[16,4096]{1,0:T(8,128)(2,1)}, u32[]{:S(2)}, u32[]{:S(2)}) collective-permute-start(bf16[16,4096]{1,0:T(8,128)(2,1)S(1)} %get-tuple-element.784), channel_id=1, source_target_pairs={{0,24},{8,16},{16,0},{24,8},{1,25},{9,17},{17,1},{25,9},{2,26},{10... | collective-permute-start | bytes 393224 | tf_op jit(solution)/shard_map/cond/branch_22_fun/ppermute | solution.py:453
  106.6 0.3 collective-permute-start.211
  106.9 4.3 %collective-permute-done.208 = bf16[16,4096]{1,0:T(8,128)(2,1)} collective-permute-done((bf16[16,4096]{1,0:T(8,128)(2,1)S(1)}, bf16[16,4096]{1,0:T(8,128)(2,1)}, u32[]{:S(2)}, u32[]{:S(2)}) %collective-permute-start.208) | collective-permute-done | bytes 131104 | tf_op jit(solution)/shard_map/cond/branch_22_fun/ppermute | solution.py:453
  111.2 2.0 %collective-permute-done.211 = bf16[2,32,1024]{2,1,0:T(8,128)(2,1)} collective-permute-done((bf16[2,32,1024]{2,1,0:T(8,128)(2,1)S(1)}, bf16[2,32,1024]{2,1,0:T(8,128)(2,1)}, u32[]{:S(2)}, u32[]{:S(2)}) %collective-permute-start.211) | collective-permute-done | bytes 131104 | tf_op jit(solution)/shard_map/cond/branch_22_fun/ppermute | solution.py:444
  113.2 1.5 %shard_map.98 = (bf16[2,32,1024]{2,1,0:T(8,128)(2,1)S(1)}, bf16[64,1024]{1,0:T(8,128)(2,1)S(1)}, bf16[64,1024]{1,0:T(8,128)(2,1)S(1)}) custom-call(f32[2,32,1024]{2,1,0:T(8,128)} %get-tuple-element.922.refs_0_, f32[64,1024]{1,0:T(8,128)} %get-tuple-element.923.refs_1_, f32[64,1024]{1,0:T(8,128)} %get-tuple-element.924.refs_2_, ...), custom_call_target="tpu_custom_call" | custom-call | flops 1 | bytes 1 | tf_op jit(solution)/shard_map/pallas_call | solution.py:482
  114.7 8.2 %conditional.7 = (bf16[2,32,1024]{2,1,0:T(8,128)(2,1)}, bf16[64,1024]{1,0:T(8,128)(2,1)}, bf16[64,1024]{1,0:T(8,128)(2,1)}) conditional(s32[]{:T(128)} %bitcast.3, (bf16[2,32,1024]{2,1,0:T(8,128)(2,1)S(1)}, bf16[64,1024]{1,0:T(8,128)(2,1)S(1)}, bf16[64,1024]{1,0:T(8,128)(2,1)S(1)}) %shard_map.98, ...), branch_computations={%region_72.0_spmd, %region_73.0_spmd, %region_74.0_spmd, %region_7... | conditional | bytes 1573008 | solution.py:456
  114.7 1.9 %collective-permute-start.282 = (bf16[2,32,1024]{2,1,0:T(8,128)(2,1)S(1)}, bf16[2,32,1024]{2,1,0:T(8,128)(2,1)}, u32[]{:S(2)}, u32[]{:S(2)}) collective-permute-start(bf16[2,32,1024]{2,1,0:T(8,128)(2,1)S(1)} %get-tuple-element.858), channel_id=1, source_target_pairs={{0,24},{8,16},{16,0},{24,8},{1,25},{9,17},{17,1},{25,9},{2,26},{10... | collective-permute-start | bytes 393224 | tf_op jit(solution)/shard_map/cond/branch_22_fun/ppermute | solution.py:453
  116.6 1.2 collective-permute-start.283
  117.8 1.0 collective-permute-start.284
  118.8 2.4 %collective-permute-done.282 = bf16[2,32,1024]{2,1,0:T(8,128)(2,1)} collective-permute-done((bf16[2,32,1024]{2,1,0:T(8,128)(2,1)S(1)}, bf16[2,32,1024]{2,1,0:T(8,128)(2,1)}, u32[]{:S(2)}, u32[]{:S(2)}) %collective-permute-start.282) | collective-permute-done | bytes 131104 | tf_op jit(solution)/shard_map/cond/branch_22_fun/ppermute | solution.py:453
  121.2 0.5 collective-permute-done.283
  121.7 1.2 collective-permute-done.284
  122.9 2.4 %shard_map.99 = (bf16[1,32,6144]{2,1,0:T(8,128)(2,1)}, bf16[1,2,128,1024]{3,2,1,0:T(8,128)(2,1)}) custom-call(s32[1]{0:T(128)S(6)} %copy.298.vis_ref, bf16[2,32,1024]{2,1,0:T(8,128)(2,1)} %get-tuple-element.932.dkv_ref, f32[2,128,1024]{2,1,0:T(8,128)} %get-tuple-element.933.down_ref, bf16[64,1024]{1,0:T(8,128)(2,1)S(1)} %get-tuple-element.934.refs_0_, ...), custom_call_target="tpu_custom_call" | custom-call | tf_op jit(solution)/shard_map/pallas_call | solution.py:629
  (29 shorter events, 0.1 us)
Async XLA Ops:
  11.6 5.9 %copy-start.9 = (s32[3]{0:T(128)S(1)}, s32[3]{0:T(128)}, u32[]{:S(2)}) copy-start(s32[3]{0:T(128)} %get-tuple-element.905.number_ref) | copy-start | bytes 40
  11.7 61.5 %all-to-all-start = ((bf16[8,32,4096]{2,1,0:T(8,128)(2,1)}), bf16[8,32,4096]{2,1,0:T(8,128)(2,1)S(1)}, u32[]{:S(2)}, u32[]{:S(2)}) async-start(bf16[8,32,4096]{2,1,0:T(8,128)(2,1)} %bitcast.13), calls=%async_computation | async-start | bytes 4194304 | tf_op jit(solution)/shard_map/all_to_all | solution.py:659
  16.8 56.3 %all-gather.3.cloned.1.call-start = ((), (), s32[]{:S(2)}) async-start(), calls=%async_computation.1 | async-start | bytes 1310720 | tf_op jit(solution)/shard_map/all_gather | solution.py:641
  17.7 30.6 %collective-permute-start.45 = (bf16[2,64,1024]{2,1,0:T(8,128)(2,1)S(1)}, bf16[2,64,1024]{2,1,0:T(8,128)(2,1)}, u32[]{:S(2)}, u32[]{:S(2)}) collective-permute-start(bf16[2,64,1024]{2,1,0:T(8,128)(2,1)S(1)} %get-tuple-element.621), channel_id=1, source_target_pairs={{0,2},{1,3},{2,0},{3,1},{4,6},{5,7},{6,4},{7,5},{8,10},{9,11},{10,... | collective-permute-start | bytes 786440 | tf_op jit(solution)/shard_map/cond/branch_22_fun/ppermute | solution.py:444
  19.7 7.3 %collective-permute-start.44 = (bf16[2,32,1024]{2,1,0:T(8,128)(2,1)S(1)}, bf16[2,32,1024]{2,1,0:T(8,128)(2,1)}, u32[]{:S(2)}, u32[]{:S(2)}) collective-permute-start(bf16[2,32,1024]{2,1,0:T(8,128)(2,1)S(1)} %get-tuple-element.620), channel_id=1, source_target_pairs={{24,0},{16,8},{0,16},{8,24},{25,1},{17,9},{1,17},{9,25},{26,2},{18... | collective-permute-start | bytes 393224 | tf_op jit(solution)/shard_map/cond/branch_22_fun/ppermute | solution.py:453
  50.1 10.9 %collective-permute-start.290 = (bf16[2,96,1024]{2,1,0:T(8,128)(2,1)}, bf16[2,96,1024]{2,1,0:T(8,128)(2,1)S(1)}, u32[]{:S(2)}, u32[]{:S(2)}) collective-permute-start(bf16[2,96,1024]{2,1,0:T(8,128)(2,1)} %shard_map.95.refs_0_), channel_id=1, source_target_pairs={{0,4},{1,5},{2,6},{3,7},{4,0},{5,1},{6,2},{7,3},{8,12},{9,13},{10,... | collective-permute-start | bytes 1179656 | tf_op jit(solution)/shard_map/ppermute | solution.py:464
  51.5 21.0 %collective-permute-start.292 = (bf16[2,96,1024]{2,1,0:T(8,128)(2,1)}, bf16[2,96,1024]{2,1,0:T(8,128)(2,1)S(1)}, u32[]{:S(2)}, u32[]{:S(2)}) collective-permute-start(bf16[2,96,1024]{2,1,0:T(8,128)(2,1)} %shard_map.95.refs_0_), channel_id=1, source_target_pairs={{0,1},{1,0},{2,3},{3,2},{4,5},{5,4},{6,7},{7,6},{8,9},{9,8},{10,11... | collective-permute-start | bytes 1179656 | tf_op jit(solution)/shard_map/ppermute | solution.py:464
  60.9 13.2 %copy-start.1 = (bf16[2,96,1024]{2,1,0:T(8,128)(2,1)}, bf16[2,96,1024]{2,1,0:T(8,128)(2,1)S(1)}, u32[]{:S(2)}) copy-start(bf16[2,96,1024]{2,1,0:T(8,128)(2,1)S(1)} %collective-permute-done.290.refs_2_) | copy-start | bytes 1179652
  60.9 12.2 %collective-permute-start.294 = (bf16[2,96,1024]{2,1,0:T(8,128)(2,1)S(1)}, bf16[2,96,1024]{2,1,0:T(8,128)(2,1)S(1)}, u32[]{:S(2)}, u32[]{:S(2)}) collective-permute-start(bf16[2,96,1024]{2,1,0:T(8,128)(2,1)S(1)} %collective-permute-done.290.refs_2_), channel_id=1, source_target_pairs={{0,1},{1,0},{2,3},{3,2},{4,5},{5,4},{6,7},{7,6},{8,9},{9,8},{10,11... | collective-permute-start | bytes 1179656 | tf_op jit(solution)/shard_map/ppermute | solution.py:464
  60.9 7.4 %collective-permute-start.291 = (bf16[2,32,1024]{2,1,0:T(8,128)(2,1)}, bf16[2,32,1024]{2,1,0:T(8,128)(2,1)S(1)}, u32[]{:S(2)}, u32[]{:S(2)}) collective-permute-start(bf16[2,32,1024]{2,1,0:T(8,128)(2,1)} %get-tuple-element.913.refs_0_), channel_id=1, source_target_pairs={{0,6},{1,7},{2,4},{3,5},{4,2},{5,3},{6,0},{7,1},{8,14},{9,15},{10,... | collective-permute-start | bytes 393224 | tf_op jit(solution)/shard_map/ppermute | solution.py:464
  62.4 8.7 %collective-permute-start.289 = (bf16[2,32,1024]{2,1,0:T(8,128)(2,1)}, bf16[2,32,1024]{2,1,0:T(8,128)(2,1)S(1)}, u32[]{:S(2)}, u32[]{:S(2)}) collective-permute-start(bf16[2,32,1024]{2,1,0:T(8,128)(2,1)} %get-tuple-element.913.refs_0_), channel_id=1, source_target_pairs={{0,2},{1,3},{2,0},{3,1},{4,6},{5,7},{6,4},{7,5},{8,10},{9,11},{10,... | collective-permute-start | bytes 393224 | tf_op jit(solution)/shard_map/ppermute | solution.py:464
  63.9 8.6 %collective-permute-start.288 = (bf16[2,64,1024]{2,1,0:T(8,128)(2,1)}, bf16[2,64,1024]{2,1,0:T(8,128)(2,1)S(1)}, u32[]{:S(2)}, u32[]{:S(2)}) collective-permute-start(bf16[2,64,1024]{2,1,0:T(8,128)(2,1)} %get-tuple-element.910), channel_id=1, source_target_pairs={{0,1},{1,2},{2,3},{3,4},{4,5},{5,6},{6,7},{8,9},{9,10},{10,11},{11... | collective-permute-start | bytes 786440 | tf_op jit(solution)/shard_map/ppermute | solution.py:577
  68.3 4.2 %copy-start.5 = (bf16[2,32,1024]{2,1,0:T(8,128)(2,1)}, bf16[2,32,1024]{2,1,0:T(8,128)(2,1)S(1)}, u32[]{:S(2)}) copy-start(bf16[2,32,1024]{2,1,0:T(8,128)(2,1)S(1)} %collective-permute-done.291.refs_3_) | copy-start | bytes 393220
  68.3 2.8 %collective-permute-start.295 = (bf16[2,32,1024]{2,1,0:T(8,128)(2,1)S(1)}, bf16[2,32,1024]{2,1,0:T(8,128)(2,1)S(1)}, u32[]{:S(2)}, u32[]{:S(2)}) collective-permute-start(bf16[2,32,1024]{2,1,0:T(8,128)(2,1)S(1)} %collective-permute-done.291.refs_3_), channel_id=1, source_target_pairs={{0,1},{1,0},{2,3},{3,2},{4,5},{5,4},{6,7},{7,6},{8,9},{9,8},{10,11... | collective-permute-start | bytes 393224 | tf_op jit(solution)/shard_map/ppermute | solution.py:464
  71.2 1.4 %copy-start.6 = (bf16[2,32,1024]{2,1,0:T(8,128)(2,1)}, bf16[2,32,1024]{2,1,0:T(8,128)(2,1)S(1)}, u32[]{:S(2)}) copy-start(bf16[2,32,1024]{2,1,0:T(8,128)(2,1)S(1)} %collective-permute-done.289.refs_1_) | copy-start | bytes 393220
  71.2 1.3 %collective-permute-start.293 = (bf16[2,32,1024]{2,1,0:T(8,128)(2,1)S(1)}, bf16[2,32,1024]{2,1,0:T(8,128)(2,1)S(1)}, u32[]{:S(2)}, u32[]{:S(2)}) collective-permute-start(bf16[2,32,1024]{2,1,0:T(8,128)(2,1)S(1)} %collective-permute-done.289.refs_1_), channel_id=1, source_target_pairs={{0,1},{1,0},{2,3},{3,2},{4,5},{5,4},{6,7},{7,6},{8,9},{9,8},{10,11... | collective-permute-start | bytes 393224 | tf_op jit(solution)/shard_map/ppermute | solution.py:464
  71.2 1.4 %copy-start.7 = (bf16[2,32,1024]{2,1,0:T(8,128)(2,1)}, bf16[2,32,1024]{2,1,0:T(8,128)(2,1)S(1)}, u32[]{:S(2)}) copy-start(bf16[2,32,1024]{2,1,0:T(8,128)(2,1)S(1)} %collective-permute-done.295.refs_7_) | copy-start | bytes 393220
  72.5 0.7 copy-start.8
  72.5 1.6 %copy-start.4 = (bf16[2,64,1024]{2,1,0:T(8,128)(2,1)}, bf16[2,64,1024]{2,1,0:T(8,128)(2,1)S(1)}, u32[]{:S(2)}) copy-start(bf16[2,64,1024]{2,1,0:T(8,128)(2,1)S(1)} %collective-permute-done.288.halo_ref) | copy-start | bytes 786436
  73.2 0.8 copy-start.2
  73.2 0.9 copy-start.3
  73.2 1.6 %copy-start = (bf16[8,32,4096]{2,1,0:T(8,128)(2,1)}, bf16[8,32,4096]{2,1,0:T(8,128)(2,1)S(1)}, u32[]{:S(2)}) copy-start(bf16[8,32,4096]{2,1,0:T(8,128)(2,1)S(1)} %all-to-all-done) | copy-start | bytes 6291460
  87.5 14.0 %copy-start.10 = (bf16[16,4096]{1,0:T(8,128)(2,1)S(1)}, bf16[16,4096]{1,0:T(8,128)(2,1)}, u32[]{:S(2)}) copy-start(bf16[16,4096]{1,0:T(8,128)(2,1)} %get-tuple-element.925) | copy-start | bytes 393220
  87.5 11.8 %collective-permute-start.115 = (bf16[2,192,1024]{2,1,0:T(8,128)(2,1)S(1)}, bf16[2,192,1024]{2,1,0:T(8,128)(2,1)}, u32[]{:S(2)}, u32[]{:S(2)}) collective-permute-start(bf16[2,192,1024]{2,1,0:T(8,128)(2,1)S(1)} %get-tuple-element.691), channel_id=1, source_target_pairs={{0,1},{1,0},{2,3},{3,2},{4,5},{5,4},{6,7},{7,6},{8,9},{9,8},{10,11... | collective-permute-start | bytes 2359304 | tf_op jit(solution)/shard_map/cond/branch_22_fun/ppermute | solution.py:444
  87.7 11.6 %collective-permute-start.116 = (bf16[2,64,1024]{2,1,0:T(8,128)(2,1)}, bf16[2,64,1024]{2,1,0:T(8,128)(2,1)}, u32[]{:S(2)}, u32[]{:S(2)}) collective-permute-start(bf16[2,64,1024]{2,1,0:T(8,128)(2,1)} %get-tuple-element.692), channel_id=1, source_target_pairs={{1,0},{2,1},{3,2},{4,3},{5,4},{6,5},{7,6},{9,8},{10,9},{11,10},{12... | collective-permute-start | bytes 786440 | tf_op jit(solution)/shard_map/cond/branch_22_fun/ppermute | solution.py:444
  89.0 10.3 %collective-permute-start.114 = (bf16[16,4096]{1,0:T(8,128)(2,1)}, bf16[16,4096]{1,0:T(8,128)(2,1)}, u32[]{:S(2)}, u32[]{:S(2)}) collective-permute-start(bf16[16,4096]{1,0:T(8,128)(2,1)} %get-tuple-element.690), channel_id=1, source_target_pairs={{0,24},{8,16},{16,0},{24,8},{1,25},{9,17},{17,1},{25,9},{2,26},{10... | collective-permute-start | bytes 393224 | tf_op jit(solution)/shard_map/cond/branch_22_fun/ppermute | solution.py:453
  101.5 11.7 %collective-permute-start.209 = (bf16[2,64,1024]{2,1,0:T(8,128)(2,1)S(1)}, bf16[2,64,1024]{2,1,0:T(8,128)(2,1)}, u32[]{:S(2)}, u32[]{:S(2)}) collective-permute-start(bf16[2,64,1024]{2,1,0:T(8,128)(2,1)S(1)} %get-tuple-element.785), channel_id=1, source_target_pairs={{0,2},{1,3},{2,0},{3,1},{4,6},{5,7},{6,4},{7,5},{8,10},{9,11},{10,... | collective-permute-start | bytes 786440 | tf_op jit(solution)/shard_map/cond/branch_22_fun/ppermute | solution.py:444
  102.8 10.4 %collective-permute-start.210 = (bf16[2,64,1024]{2,1,0:T(8,128)(2,1)S(1)}, bf16[2,64,1024]{2,1,0:T(8,128)(2,1)}, u32[]{:S(2)}, u32[]{:S(2)}) collective-permute-start(bf16[2,64,1024]{2,1,0:T(8,128)(2,1)S(1)} %get-tuple-element.786), channel_id=1, source_target_pairs={{0,4},{1,5},{2,6},{3,7},{4,0},{5,1},{6,2},{7,3},{8,12},{9,13},{10,... | collective-permute-start | bytes 786440 | tf_op jit(solution)/shard_map/cond/branch_22_fun/ppermute | solution.py:444
  104.1 7.1 %collective-permute-start.208 = (bf16[16,4096]{1,0:T(8,128)(2,1)S(1)}, bf16[16,4096]{1,0:T(8,128)(2,1)}, u32[]{:S(2)}, u32[]{:S(2)}) collective-permute-start(bf16[16,4096]{1,0:T(8,128)(2,1)S(1)} %get-tuple-element.784), channel_id=1, source_target_pairs={{0,24},{8,16},{16,0},{24,8},{1,25},{9,17},{17,1},{25,9},{2,26},{10... | collective-permute-start | bytes 393224 | tf_op jit(solution)/shard_map/cond/branch_22_fun/ppermute | solution.py:453
  106.6 6.6 %collective-permute-start.211 = (bf16[2,32,1024]{2,1,0:T(8,128)(2,1)S(1)}, bf16[2,32,1024]{2,1,0:T(8,128)(2,1)}, u32[]{:S(2)}, u32[]{:S(2)}) collective-permute-start(bf16[2,32,1024]{2,1,0:T(8,128)(2,1)S(1)} %get-tuple-element.787), channel_id=1, source_target_pairs={{0,6},{1,7},{2,4},{3,5},{4,2},{5,3},{6,0},{7,1},{8,14},{9,15},{10,... | collective-permute-start | bytes 393224 | tf_op jit(solution)/shard_map/cond/branch_22_fun/ppermute | solution.py:444
  114.7 6.5 %collective-permute-start.282 = (bf16[2,32,1024]{2,1,0:T(8,128)(2,1)S(1)}, bf16[2,32,1024]{2,1,0:T(8,128)(2,1)}, u32[]{:S(2)}, u32[]{:S(2)}) collective-permute-start(bf16[2,32,1024]{2,1,0:T(8,128)(2,1)S(1)} %get-tuple-element.858), channel_id=1, source_target_pairs={{0,24},{8,16},{16,0},{24,8},{1,25},{9,17},{17,1},{25,9},{2,26},{10... | collective-permute-start | bytes 393224 | tf_op jit(solution)/shard_map/cond/branch_22_fun/ppermute | solution.py:453
  116.6 5.1 %collective-permute-start.283 = (bf16[64,1024]{1,0:T(8,128)(2,1)S(1)}, bf16[64,1024]{1,0:T(8,128)(2,1)}, u32[]{:S(2)}, u32[]{:S(2)}) collective-permute-start(bf16[64,1024]{1,0:T(8,128)(2,1)S(1)} %get-tuple-element.859), channel_id=1, source_target_pairs={{0,2},{1,3},{2,0},{3,1},{4,6},{5,7},{6,4},{7,5},{8,10},{9,11},{10,... | collective-permute-start | bytes 393224 | tf_op jit(solution)/shard_map/cond/branch_22_fun/ppermute | solution.py:444
  117.8 5.1 %collective-permute-start.284 = (bf16[64,1024]{1,0:T(8,128)(2,1)S(1)}, bf16[64,1024]{1,0:T(8,128)(2,1)}, u32[]{:S(2)}, u32[]{:S(2)}) collective-permute-start(bf16[64,1024]{1,0:T(8,128)(2,1)S(1)} %get-tuple-element.860), channel_id=1, source_target_pairs={{0,4},{1,5},{2,6},{3,7},{4,0},{5,1},{6,2},{7,3},{8,12},{9,13},{10,... | collective-permute-start | bytes 393224 | tf_op jit(solution)/shard_map/cond/branch_22_fun/ppermute | solution.py:444
Sparse Core Ops, SparseCore 0:
  19.8 29.6 all-gather.2
